TPU v7x, 256 devices: a whole 4x4x8 slice. The times are simulated.
256 devices in a mesh: dom: 32 (over z, x), band: 8 (over y, core).
Axes of the slice: x: 4, y: 4, z: 8, core: 2. Of those that a mesh axis runs over, the one named last changes fastest.
Arguments:
- orbitals: bfloat16 [128, 256, 32, 128], P('band', 'dom'), may hold values from -6 to 6
- potential: float32 [256, 32, 128], P('dom'), may hold values from -6 to 6
- coupling: float32 [8, 8], replicated, may hold values from -2 to 2
- projectors: bfloat16 [8192, 512], P('dom'), may hold values from -1.1953125 to 1.1953125
- slot_atom: int32 [8192], P('dom'), may hold values from 0 to 2047, as said below
- slot_domain_block: int32 [8192], P('dom'), may hold values from 0 to 511
- slot_count: int32 [32], P('dom'), may hold values from 64 to 256
Outputs:
- applied: bfloat16 [128, 256, 32, 128], P('band', 'dom')
- subspace: float32 [128, 128], P('band')
Inputs may be any that keep to these rules, and one draw needn't show every extreme that they name: `slot_atom`: every slot of domain d names an atom whose owner, atom // 64, is d - 1, d or d + 1, counted cyclically over the 32 domains.
All inputs are finite; a program needn't handle non-finite values.
Results may differ from a plain program's by a relative error of at most 0.0038.
Values may be sent and summed in bfloat16 or wider, within the bound.
A program may use at most 128 MiB of HBM per device.

v0:
```python
import jax
import jax.numpy as jnp
from jax import lax
from jax.sharding import PartitionSpec as P

ATOM_PROJECTORS = 8
BLOCK_POINTS = 64
ATOMS_PER_DOMAIN = 64


STENCIL = (-205.0 / 72.0, 8.0 / 5.0, -1.0 / 5.0, 8.0 / 315.0, -1.0 / 560.0)


def padded_2(block, sides, width):
    for axis, dim in sides:
        count = lax.axis_size(axis)
        forward = [(i, i + 1) for i in range(count - 1)]
        forward.append((count - 1, 0))
        backward = [(target, source) for source, target in forward]
        low = lax.ppermute(
            lax.slice_in_dim(block, block.shape[dim] - width, None, axis=dim), axis, forward
        )
        high = lax.ppermute(lax.slice_in_dim(block, 0, width, axis=dim), axis, backward)
        block = jnp.concatenate([low, block, high], axis=dim)
    return block


def from_behind(block, axis, distance):
    devices = range(lax.axis_size(axis))
    route = [((i - distance) % len(devices), i) for i in devices]
    return lax.ppermute(block, axis, route)


def couple(coefficients, coupling, own_orbs):
    atom_rows = coefficients.shape[0]
    reshaped_array = coefficients.reshape(atom_rows, ATOM_PROJECTORS, own_orbs)
    mixed_rows = jnp.einsum(
        "pj,ajo->apo", coupling, reshaped_array, precision=lax.Precision.HIGHEST
    )
    return mixed_rows.astype(jnp.bfloat16).reshape(atom_rows, ATOM_PROJECTORS * own_orbs)


def local(orbitals, potential, coupling, projectors, slot_atom, slot_domain_block, slot_count):
    own_orbs, planes, rows_y, rows_z = orbitals.shape
    points = planes * rows_y * rows_z
    blocks_dom = points // BLOCK_POINTS
    slot_total = slot_atom.shape[0]
    padded = padded_2(orbitals, (("dom", 1),), 4)
    values = padded.astype(jnp.float32)
    center = values[:, 4 : 4 + planes]
    summed = 3.0 * STENCIL[0] * center
    for offset in range(1, 5):
        summed = summed + STENCIL[offset] * (
            values[:, 4 - offset : 4 - offset + planes]
            + values[:, 4 + offset : 4 + offset + planes]
        )
    for dimension in (2, 3):
        for offset in range(1, 5):
            summed = summed + STENCIL[offset] * (
                jnp.roll(center, offset, dimension) + jnp.roll(center, -offset, dimension)
            )
    local_part = -0.5 * summed + potential[None] * center
    live_mask = (jnp.arange(slot_total, dtype=jnp.int32) < slot_count[0]).astype(jnp.float32)
    reshaped_array = projectors.reshape(slot_total, ATOM_PROJECTORS, BLOCK_POINTS)
    flat_orbs = orbitals.reshape(own_orbs, blocks_dom, BLOCK_POINTS)
    picked = jnp.take(flat_orbs, slot_domain_block, axis=1)
    slot_coef = (
        jnp.einsum("spk,osk->spo", reshaped_array, picked, preferred_element_type=jnp.float32)
        * live_mask[:, None, None]
    )
    slot_coef = slot_coef.reshape(slot_total, ATOM_PROJECTORS * own_orbs)
    domain_count = lax.axis_size("dom")
    dom_index = lax.axis_index("dom")
    window = (
        slot_atom // ATOMS_PER_DOMAIN - dom_index + 1 + domain_count
    ) % domain_count * ATOMS_PER_DOMAIN + slot_atom % ATOMS_PER_DOMAIN
    partial_value = jax.ops.segment_sum(slot_coef, window, num_segments=3 * ATOMS_PER_DOMAIN)
    from_upper = from_behind(partial_value[:ATOMS_PER_DOMAIN], "dom", -1)
    from_lower = from_behind(partial_value[2 * ATOMS_PER_DOMAIN :], "dom", 1)
    owned_rows = partial_value[ATOMS_PER_DOMAIN : 2 * ATOMS_PER_DOMAIN] + from_upper + from_lower
    extended = padded_2(couple(owned_rows, coupling, own_orbs), (("dom", 0),), ATOMS_PER_DOMAIN)
    spread = extended[window]
    spread = spread.reshape(slot_total, ATOM_PROJECTORS, own_orbs)
    contrib = (
        jnp.einsum("spk,spo->sok", reshaped_array, spread, preferred_element_type=jnp.float32)
        * live_mask[:, None, None]
    )
    projected = jax.ops.segment_sum(contrib, slot_domain_block, num_segments=blocks_dom)
    projected = jnp.transpose(projected, (1, 0, 2)).reshape(own_orbs, planes, rows_y, rows_z)
    applied = (local_part + projected).astype(jnp.bfloat16)
    orb_flat = orbitals.reshape(own_orbs, points)
    image_flat = applied.reshape(own_orbs, points)
    orb_all, image_all = (
        lax.all_to_all(orb_flat, "band", split_axis=1, concat_axis=0, tiled=True),
        lax.all_to_all(image_flat, "band", split_axis=1, concat_axis=0, tiled=True),
    )
    full_gram = lax.dot_general(
        orb_all, image_all, (((1,), (1,)), ((), ())), preferred_element_type=jnp.float32
    )
    partial_gram = lax.psum_scatter(
        full_gram.astype(jnp.bfloat16), "band", scatter_dimension=0, tiled=True
    ).astype(jnp.float32)
    gram_matrix = lax.psum(partial_gram, "dom") / float(points * domain_count)
    return (applied, gram_matrix)


def solution(mesh):
    return jax.shard_map(
        local,
        mesh=mesh,
        in_specs=(
            P("band", "dom", None, None),
            P("dom", None, None),
            P(),
            P("dom", None),
            P("dom"),
            P("dom"),
            P("dom"),
        ),
        out_specs=(P("band", "dom", None, None), P("band", None)),
        check_vma=False,
    )
```

profile of v0, /device:TPU:0, one launch (start us, length us, event | category | flops | bytes accessed | tf_op | source)
XLA Modules:
  0.0 344.5 jit_solution(9107897452730883616)
XLA Ops:
  7.2 0.0 copy-start
  7.2 1.1 copy.45
  8.3 0.3 copy.46
  8.6 2.9 reshape.46
  11.5 0.0 copy-start.6
  11.6 2.7 copy.44
  14.9 3.3 gather_fusion
  18.3 2.8 fusion.28
  21.1 0.4 copy.47
  21.5 0.1 copy.48
  21.6 1.4 scatter_custom_fusion
  23.1 0.1 collective-permute-start.3
  23.2 6.4 %collective-permute-start.2 = (f32[64,128]{1,0:T(8,128)S(1)}, f32[64,128]{1,0:T(8,128)S(1)}, u32[]{:S(2)}, u32[]{:S(2)}) collective-permute-start(f32[64,128]{1,0:T(8,128)S(1)} %get-tuple-element.46), channel_id=1, source_target_pairs={{8,0},{16,8},{24,16},{32,24},{40,32},{48,40},{56,48},{64,56},{72,6... | collective-permute-start | bytes 98312 | tf_op jit(solution)/shard_map/ppermute | solution.py:31
  29.6 1.1 fusion.60
  30.7 1.9 collective-permute-start.1
  32.6 0.1 collective-permute-start
  32.7 0.5 reshape.90
  33.2 1.6 copy.62
  34.8 4.5 %all-to-all-start.1 = ((bf16[16,8,4096]{2,0,1:T(8,128)(2,1)}), bf16[16,8,4096]{2,0,1:T(8,128)(2,1)}, u32[]{:S(2)}, u32[]{:S(2)}) async-start(bf16[16,8,4096]{2,0,1:T(8,128)(2,1)} %copy.62), calls=%async_computation.1 | async-start | bytes 2097152 | tf_op jit(solution)/shard_map/all_to_all | solution.py:94
  39.3 0.0 reduce-scatter.4.cloned.1.call-start
  39.3 0.1 copy.49
  39.4 0.2 fusion.29
  39.7 0.1 copy.52
  39.8 5.3 %collective-permute-start.5 = (bf16[64,128]{1,0:T(8,128)(2,1)S(1)}, bf16[64,128]{1,0:T(8,128)(2,1)S(1)}, u32[]{:S(2)}, u32[]{:S(2)}) collective-permute-start(bf16[64,128]{1,0:T(8,128)(2,1)S(1)} %copy.52), channel_id=1, source_target_pairs={{8,0},{16,8},{24,16},{32,24},{40,32},{48,40},{56,48},{64,56},{72,6... | collective-permute-start | bytes 49160 | tf_op jit(solution)/shard_map/ppermute | solution.py:23
  45.1 1.4 collective-permute-done.5
  46.5 5.6 %collective-permute-done.4 = bf16[64,128]{1,0:T(8,128)(2,1)S(1)} collective-permute-done((bf16[64,128]{1,0:T(8,128)(2,1)S(1)}, bf16[64,128]{1,0:T(8,128)(2,1)S(1)}, u32[]{:S(2)}, u32[]{:S(2)}) %collective-permute-start.4) | collective-permute-done | bytes 16416 | tf_op jit(solution)/shard_map/ppermute | solution.py:20
  52.1 0.9 gather_fusion.1
  53.0 0.1 copy.55
  53.1 1.1 copy.56
  54.2 1.9 convolution_multiply_fusion
  56.1 2.2 broadcast_in_dim.30
  58.3 28.0 %scatter_fusion = f32[512,16,64]{2,1,0:T(8,128)} fusion(f32[512,16,64]{2,1,0:T(8,128)} %broadcast_in_dim.30, s32[256]{0:T(256)S(1)} %copy-done.6, f32[256,16,64]{2,1,0:T(8,128)S(1)} %convolution_multiply_fusion), kind=kCustom, calls=%fused_computation.3 | custom fusion | flops 262144 | bytes 3146752 | tf_op jit(solution)/shard_map/scatter-add | solution.py:88
  86.3 5.6 %copy.58 = f32[16,512,64]{2,1,0:T(8,128)} copy(f32[16,512,64]{2,0,1:T(8,128)} %bitcast.38) | data formatting | bytes 4194304 | tf_op jit(solution)/shard_map/transpose | solution.py:89
  91.9 3.3 reshape.52
  95.2 1.5 maximum_convert_fusion
  96.7 0.8 fusion.58
  97.5 0.8 fusion.59
  98.2 2.7 fusion.56
  100.9 2.7 fusion.57
  103.6 2.7 fusion.54
  106.3 2.7 fusion.55
  109.1 2.7 fusion.52
  111.7 2.7 fusion.53
  114.5 0.1 fusion.50
  114.6 2.5 fusion.51
  117.1 0.1 fusion.48
  117.3 2.5 fusion.49
  119.8 0.1 fusion.46
  119.9 2.6 fusion.47
  122.5 2.5 fusion.45
  125.1 0.1 maximum_convert_fusion.2
  125.2 0.8 copy-done.5
  126.0 16.2 %fusion.27 = bf16[16,8,32,128]{3,2,1,0:T(8,128)(2,1)S(1)} fusion(f32[16,8,32,128]{3,2,1,0:T(8,128)S(1)} %reshape.52, f32[16,8,32,4]{3,2,1,0:T(8,128)S(1)} %get-tuple-element.39, f32[16,8,32,124]{3,2,1,0:T(8,128)S(1)} %get-tuple-element.41, f32[16,8,32,124]{3,2,1,0:T(8,128)S(1)} %get-tuple-element.40, f32[16,8,32,4]{3,2,1,0:T(8,128)S(1)} %get-tuple-element.38, ...), kind=kLoop, calls=%fused_computation.44 | loop fusion | flops 30408704 | bytes 55705600 | tf_op jit(solution)/shard_map/convert_element_type | solution.py:90
  142.2 0.0 copy-start.4
  142.2 0.5 all_to_all.28
  142.7 0.6 copy.59
  143.3 20.7 %all_to_all.38 = bf16[16,8,4096]{2,0,1:T(8,128)(2,1)S(1)} all-to-all(bf16[16,8,4096]{2,0,1:T(8,128)(2,1)S(1)} %copy.59), channel_id=1, replica_groups=mesh['dom'=32,'band'=8] {'band'}, dimensions={1} | all-to-all | bytes 2097152 | tf_op jit(solution)/shard_map/all_to_all | solution.py:95
  164.0 1.7 fusion.30
  165.6 0.7 copy.63
  166.4 0.0 reduce-scatter.4.cloned.1.call-update
  166.4 26.7 %reduce-scatter.4.cloned.1.call-done = bf16[16,128]{1,0:T(8,128)(2,1)} async-done(((bf16[128,128]{1,0:T(8,128)(2,1)}), bf16[16,128]{1,0:T(8,128)(2,1)}) %reduce-scatter.4.cloned.1.call-update) | async-done | bytes 4112
  193.1 0.8 copy.64
  193.9 143.1 %psum.7 = f32[16,128]{0,1:T(8,128)S(1)} all-reduce(bf16[16,128]{0,1:T(8,128)(2,1)S(1)} %copy.64), channel_id=1, replica_groups=mesh['dom'=32,'band'=8] {'dom'}, use_global_device_ids=true, to_apply=%region_3.4 | all-reduce | flops 2048 | bytes 12288 | tf_op jit(solution)/shard_map/psum | solution.py:103
  337.0 0.7 copy.61
  (28 shorter events, 0.1 us)
Async XLA Ops:
  7.2 32.3 %copy-start = (f32[8,8]{1,0:T(8,128)S(1)}, f32[8,8]{1,0:T(8,128)}, u32[]{:S(2)}) copy-start(f32[8,8]{1,0:T(8,128)} %param.9) | copy-start | bytes 772
  8.6 9.7 %copy-start.3 = (bf16[256,8,64]{2,1,0:T(8,128)(2,1)}, bf16[256,8,64]{2,1,0:T(8,128)(2,1)S(1)}, u32[]{:S(2)}) copy-start(bf16[256,8,64]{2,1,0:T(8,128)(2,1)S(1)} %copy.46) | copy-start | bytes 786436
  11.5 2.7 copy-start.6
  18.3 3.3 copy-start.7
  18.3 11.3 %copy-start.2 = (bf16[16,8,32,128]{3,2,1,0:T(8,128)(2,1)S(1)}, bf16[16,8,32,128]{3,2,1,0:T(8,128)(2,1)}, u32[]{:S(2)}) copy-start(bf16[16,8,32,128]{3,2,1,0:T(8,128)(2,1)} %param.7) | copy-start | bytes 3145732
  23.1 16.2 %collective-permute-start.3 = (f32[64,128]{1,0:T(8,128)S(1)}, f32[64,128]{1,0:T(8,128)S(1)}, u32[]{:S(2)}, u32[]{:S(2)}) collective-permute-start(f32[64,128]{1,0:T(8,128)S(1)} %get-tuple-element.47), channel_id=1, source_target_pairs={{248,0},{0,8},{8,16},{16,24},{24,32},{32,40},{40,48},{48,56},{56,6... | collective-permute-start | bytes 98312 | tf_op jit(solution)/shard_map/ppermute | solution.py:31
  23.2 16.2 %collective-permute-start.2 = (f32[64,128]{1,0:T(8,128)S(1)}, f32[64,128]{1,0:T(8,128)S(1)}, u32[]{:S(2)}, u32[]{:S(2)}) collective-permute-start(f32[64,128]{1,0:T(8,128)S(1)} %get-tuple-element.46), channel_id=1, source_target_pairs={{8,0},{16,8},{24,16},{32,24},{40,32},{48,40},{56,48},{64,56},{72,6... | collective-permute-start | bytes 98312 | tf_op jit(solution)/shard_map/ppermute | solution.py:31
  30.7 64.5 %collective-permute-start.1 = (bf16[16,4,32,128]{3,2,1,0:T(8,128)(2,1)}, bf16[16,4,32,128]{3,2,1,0:T(8,128)(2,1)}, u32[]{:S(2)}, u32[]{:S(2)}) collective-permute-start(bf16[16,4,32,128]{3,2,1,0:T(8,128)(2,1)} %get-tuple-element.45), channel_id=1, source_target_pairs={{8,0},{16,8},{24,16},{32,24},{40,32},{48,40},{56,48},{64,56},{72,6... | collective-permute-start | bytes 1572872 | tf_op jit(solution)/shard_map/ppermute | solution.py:23
  32.6 62.5 %collective-permute-start = (bf16[16,4,32,128]{3,2,1,0:T(8,128)(2,1)}, bf16[16,4,32,128]{3,2,1,0:T(8,128)(2,1)}, u32[]{:S(2)}, u32[]{:S(2)}) collective-permute-start(bf16[16,4,32,128]{3,2,1,0:T(8,128)(2,1)} %get-tuple-element.44), channel_id=1, source_target_pairs={{0,8},{8,16},{16,24},{24,32},{32,40},{40,48},{48,56},{56,64},{64,7... | collective-permute-start | bytes 1572872 | tf_op jit(solution)/shard_map/ppermute | solution.py:20
  34.8 108.5 %all-to-all-start.1 = ((bf16[16,8,4096]{2,0,1:T(8,128)(2,1)}), bf16[16,8,4096]{2,0,1:T(8,128)(2,1)}, u32[]{:S(2)}, u32[]{:S(2)}) async-start(bf16[16,8,4096]{2,0,1:T(8,128)(2,1)} %copy.62), calls=%async_computation.1 | async-start | bytes 2097152 | tf_op jit(solution)/shard_map/all_to_all | solution.py:94
  39.3 153.8 %reduce-scatter.4.cloned.1.call-start = ((), (), s32[]{:S(2)}) async-start(), calls=%async_computation.3 | async-start | bytes 36864
  39.8 6.8 %collective-permute-start.5 = (bf16[64,128]{1,0:T(8,128)(2,1)S(1)}, bf16[64,128]{1,0:T(8,128)(2,1)S(1)}, u32[]{:S(2)}, u32[]{:S(2)}) collective-permute-start(bf16[64,128]{1,0:T(8,128)(2,1)S(1)} %copy.52), channel_id=1, source_target_pairs={{8,0},{16,8},{24,16},{32,24},{40,32},{48,40},{56,48},{64,56},{72,6... | collective-permute-start | bytes 49160 | tf_op jit(solution)/shard_map/ppermute | solution.py:23
  45.1 7.1 %collective-permute-start.4 = (bf16[64,128]{1,0:T(8,128)(2,1)S(1)}, bf16[64,128]{1,0:T(8,128)(2,1)S(1)}, u32[]{:S(2)}, u32[]{:S(2)}) collective-permute-start(bf16[64,128]{1,0:T(8,128)(2,1)S(1)} %copy.52), channel_id=1, source_target_pairs={{0,8},{8,16},{16,24},{24,32},{32,40},{40,48},{48,56},{56,64},{64,7... | collective-permute-start | bytes 49160 | tf_op jit(solution)/shard_map/ppermute | solution.py:20
  125.1 0.9 copy-start.5
  142.2 1.1 copy-start.4
  142.7 194.9 %copy-start.1 = (f32[8,8]{1,0:T(8,128)S(1)}, f32[8,8]{1,0:T(8,128)}, u32[]{:S(2)}) copy-start(f32[8,8]{1,0:T(8,128)} %param.9) | copy-start | bytes 772
Sparse Core Ops, SparseCore 0:
  166.5 26.5 reduce-scatter.3
where the time goes:
time: 346 us; the launch traced here: 344 us
  blocking collectives  164 us (47%)
  local copies, waits for them, and re-layouts  59.7 us (17%)
  other arithmetic  47.3 us (14%)
  waiting for transfers between devices  33.8 us (10%)
  starting transfers between devices  18.3 us (5%)
  between operations  15 us (4%)
  matrix products  6.6 us (2%)
    psum x1, blocking collectives, local(): gram_matrix = lax.psum(partial_gram, 'dom') / float(points * domain_count)  143 us
    slice x15, local copies, waits for them, and re-layouts, local(): jnp.roll(center, offset, dimension) + jnp.roll(center, -offset, dimension)  28.3 us
    scatter-add x1, other arithmetic, local(): jax.ops.segment_sum(contrib, slot_domain_block, num_segments=blocks_dom)  28 us
    unnamed x2, waiting for transfers between devices  26.7 us
    all_to_all x1, blocking collectives, local(): lax.all_to_all(image_flat, 'band', split_axis=1, concat_axis=0, tiled=True)  20.7 us
    convert_element_type x1, other arithmetic, local(): applied = (local_part + projected).astype(jnp.bfloat16)  16.2 us
    ppermute x2, starting transfers between devices, padded_2(): lax.ppermute(lax.slice_in_dim(block, 0, width, axis=dim), axis, backward)  7.27 us
  transfers between devices with their start and end apart: 8, of which 3 were waited for; matrix products, arithmetic and copies ran while one was open for 27% of the time, Pallas kernels for 0%

commit v1 on v0

v1 whole, which is shorter than its diff:
```python
import functools

import jax
import jax.numpy as jnp
from jax import lax
from jax.experimental import pallas as pl
from jax.experimental.pallas import tpu as pltpu
from jax.sharding import PartitionSpec as P

MESH = pl.DeviceIdType.MESH
F32 = jnp.float32
BF16 = jnp.bfloat16
STENCIL = (-205.0 / 72.0, 8.0 / 5.0, -1.0 / 5.0, 8.0 / 315.0, -1.0 / 560.0)
ALONG_X = 4
NN = (((1,), (0,)), ((), ()))
NT = (((1,), (1,)), ((), ()))
ORDER = (3, 4, 2, 5, 1, 6, 0, 7)


def mm(a, b, dims=NN):
    return lax.dot_general(a, b, dims, preferred_element_type=F32)


def iota(shape, dim):
    return lax.broadcasted_iota(jnp.int32, shape, dim)


def one(mask):
    return jnp.where(mask, 1.0, 0.0).astype(BF16)


def split(value):
    high = value.astype(BF16)
    return high, (value - high.astype(F32)).astype(BF16)


def plane_matrix():
    r, c = iota((256, 256), 0), iota((256, 256), 1)
    same_plane, same_row = (r >> 5) == (c >> 5), (r & 31) == (c & 31)
    apart, turn = jnp.abs((r >> 5) - (c >> 5)), ((r & 31) - (c & 31)) & 31
    value = jnp.where(r == c, -1.5 * STENCIL[0], 0.0)
    for k in range(1, 5):
        value = jnp.where(same_plane & ((turn == k) | (turn == 32 - k)), -0.5 * STENCIL[k], value)
        value = jnp.where(same_row & (apart == k), -0.5 * STENCIL[k], value)
    return value


def lane_matrix():
    turn = (iota((128, 128), 0) - iota((128, 128), 1)) & 127
    value = jnp.zeros((128, 128), F32)
    for k in range(1, 5):
        value = jnp.where((turn == k) | (turn == 128 - k), -0.5 * STENCIL[k], value)
    return value


def kernel(
    domains, bands,
    v, pot, coupling, proj, atom, block, count,
    out, gram_out,
    vt, va, wt, wa, low, high, acc, gt, gm, hm, at, pt, cf, sp, q, rq, pm, lm, zm, gram, rb, rx, rz,
    barrier_unused, v_send, v_recv, w_send, w_recv, h_send, h_recv, q_send, q_recv, s_send, s_recv, own_sem,
):
    dom, band = lax.axis_index("dom"), lax.axis_index("band")
    x, z = lax.rem(dom, ALONG_X), dom // ALONG_X
    rows_z = domains // ALONG_X

    def dom_at(step):
        return {"dom": lax.rem(dom + step + domains, domains)}

    def band_at(step):
        return {"band": lax.rem(band + step, bands)}

    def x_at(step):
        return {"dom": z * ALONG_X + lax.rem(x + step, ALONG_X)}

    def z_at(step):
        return {"dom": lax.rem(z + step, rows_z) * ALONG_X + x}

    peers = [dom_at(step) for step in (1, -1, 2, -2)]
    peers += [band_at(step) for step in range(1, bands)]
    peers += [x_at(step) for step in range(1, ALONG_X)]
    peers += [z_at(step) for step in range(1, rows_z)]
    barrier = pltpu.get_barrier_semaphore()
    for peer in peers:
        pl.semaphore_signal(barrier, inc=1, device_id=peer, device_id_type=MESH)

    def send(src, dst, send_sem, recv_sem, peer):
        copy = pltpu.make_async_remote_copy(
            src_ref=src, dst_ref=dst, send_sem=send_sem, recv_sem=recv_sem, device_id=peer, device_id_type=MESH
        )
        copy.start()
        return copy

    r, c = iota((256, 256), 0), iota((256, 256), 1)
    pm[...] = one(((r & 15) == (c >> 4)) & ((r >> 4) == (c & 15)))

    def turned(piece, target, half, position):
        tiles = mm(pm[...], piece.reshape(256, 128)).astype(BF16).reshape(16, 16, 128)
        for row in range(16):
            target[4 * half + row // 4, :, pl.ds((position * 4 + row % 4) * 128, 128)] = tiles[row]

    for position, plane in enumerate(ORDER):
        for half in range(2):
            turned(v[:, plane, 16 * half : 16 * half + 16, :], vt, half, position)

    pl.semaphore_wait(barrier, len(peers))

    v_copies = []
    for step in range(1, bands):
        peer = band_at(step)
        v_copies.append(send(vt.at[peer["band"]], va.at[band], v_send.at[step - 1], v_recv.at[step - 1], peer))
    h_copies = []
    for k in range(1, 5):
        h_copies.append((
            send(v.at[:, 8 - k], low.at[4 - k], h_send.at[0, k - 1], h_recv.at[0, k - 1], dom_at(1)),
            send(v.at[:, k - 1], high.at[k - 1], h_send.at[1, k - 1], h_recv.at[1, k - 1], dom_at(-1)),
        ))
    own_v = pltpu.make_async_copy(vt.at[band], va.at[band], own_sem.at[0])
    own_v.start()

    half_of = block[...] & 1
    live = iota((1, 256), 1) < count[0]
    gt[...] = one((r == (block[...] >> 1)) & live)
    eye = one(r == c)
    gm[...] = mm(eye, gt[...], NT).astype(BF16)
    hm[...] = mm(eye, one((iota((128, 256), 0) >> 6) == half_of), NT)
    window = (((atom[...] >> 6) - dom + 1 + domains) & (domains - 1)) * 64 + (atom[...] & 63)
    at[...] = one(iota((192, 256), 0) == window)
    small_eye = one(iota((128, 128), 0) == iota((128, 128), 1))
    for pair in range(4):
        pt[2 * pair : 2 * pair + 2] = mm(small_eye, proj[:, 128 * pair : 128 * pair + 128], NT).reshape(2, 64, 256)
    fold = one((iota((64, 128), 1) & 63) == iota((64, 128), 0))

    @pl.loop(0, 16)
    def _(o):
        picked = (mm(gm[...], v[o].reshape(256, 128)) * hm[...]).astype(BF16)
        points = mm(fold, picked, NT)
        for p in range(8):
            cf[p, pl.ds(o, 1), :] = jnp.sum(points * pt[p], axis=0, keepdims=True)

    rest = cf[...].reshape(128, 256)
    total = jnp.zeros((192, 128), F32)
    for _ in range(3):
        part = rest.astype(BF16)
        rest = rest - part.astype(F32)
        total = total + mm(at[...], part, NT)
    q[...] = total.reshape(3, 64, 128)
    q_copies = [
        send(q.at[pl.ds(1, 2)], rq.at[pl.ds(1, 2)], q_send.at[0], q_recv.at[0], dom_at(1)),
        send(q.at[pl.ds(0, 2)], rq.at[pl.ds(3, 2)], q_send.at[1], q_recv.at[1], dom_at(-1)),
        send(q.at[2], rq.at[0], q_send.at[2], q_recv.at[2], dom_at(2)),
        send(q.at[0], rq.at[5], q_send.at[3], q_recv.at[3], dom_at(-2)),
    ]

    lm[0:256], lm[256:512] = split(plane_matrix())
    zm[:, 0:128], zm[:, 128:256] = split(lane_matrix())

    @pl.loop(0, 16)
    def _(o):
        values = v[o].reshape(256, 128)
        both = mm(lm[...], values)
        lanes = mm(values, zm[...])
        summed = both[0:256] + both[256:512] + lanes[:, 0:128] + lanes[:, 128:256]
        acc[o] = (summed + pot[...].reshape(256, 128) * values.astype(F32)).reshape(8, 32, 128)

    rows = []
    for p in range(8):
        line = jnp.zeros((16, 128), F32)
        for j in range(8):
            line = jnp.where((iota((16, 128), 1) >> 4) == j, coupling[p, j], line)
        rows.append(jnp.where((iota((16, 128), 1) & 15) == iota((16, 128), 0), line, 0.0))
    mixing = jnp.concatenate(rows, axis=0)

    for copy in q_copies:
        copy.wait_recv()
    owned = jnp.concatenate([rq[0] + rq[1] + q[0], rq[2] + q[1] + rq[3], q[2] + rq[4] + rq[5]], axis=0)
    coupled = lax.dot_general(mixing, owned, NT, precision=lax.Precision.HIGHEST, preferred_element_type=F32)
    sp[...] = mm(coupled.astype(BF16), at[...]).reshape(8, 16, 256)

    @pl.loop(0, 16)
    def _(o):
        added = pt[0] * sp[0, pl.ds(o, 1), :]
        for p in range(1, 8):
            added = added + pt[p] * sp[p, pl.ds(o, 1), :]
        placed = jnp.concatenate([jnp.where(half_of == 0, added, 0.0), jnp.where(half_of == 1, added, 0.0)], axis=0)
        first, second = split(placed)
        acc[o] = acc[o] + (mm(gt[...], first, NT) + mm(gt[...], second, NT)).reshape(8, 32, 128)

    w_copies = []
    for k in range(1, 5):
        for copy in h_copies[k - 1]:
            copy.wait_recv()
        for side in range(2):
            plane = 3 + k if side else 4 - k
            for half in range(2):
                span = slice(16 * half, 16 * half + 16)
                value = acc[:, plane, span, :]
                for near in range(k):
                    halo = high[near, :, span, :] if side else low[3 - near, :, span, :]
                    reach = 8 + near - plane if side else plane + 1 + near
                    value = value - 0.5 * STENCIL[reach] * halo.astype(F32)
                value = value.astype(BF16)
                out[:, plane, span, :] = value
                turned(value, wt, half, 2 * (k - 1) + side)
        span = pl.ds((k - 1) * 1024, 1024)
        step_copies = []
        for step in range(1, bands):
            peer = band_at(step)
            step_copies.append(send(
                wt.at[peer["band"], :, span], wa.at[band, :, span],
                w_send.at[k - 1, step - 1], w_recv.at[k - 1, step - 1], peer,
            ))
        w_copies.append(step_copies)
        wa[band, :, span] = wt[band, :, span]

    for copy in v_copies:
        copy.wait_recv()
    own_v.wait()
    for k in range(1, 5):
        for copy in w_copies[k - 1]:
            copy.wait_recv()
        span = slice((k - 1) * 1024, k * 1024)
        part = mm(va[:, :, span].reshape(128, 1024), wa[:, :, span].reshape(128, 1024), NT)
        gram[...] = part if k == 1 else gram[...] + part

    s_copies = []
    for step in range(1, bands):
        peer = band_at(step)
        s_copies.append(send(
            gram.at[pl.ds(pl.multiple_of(peer["band"] * 16, 16), 16)], rb.at[band],
            s_send.at[step - 1], s_recv.at[step - 1], peer,
        ))
    rb[band] = gram[pl.ds(pl.multiple_of(band * 16, 16), 16)]
    for copy in s_copies:
        copy.wait_recv()
    rx[x] = jnp.sum(rb[...], axis=0)
    x_copies = [
        send(rx.at[x], rx.at[x], s_send.at[6 + step], s_recv.at[6 + step], x_at(step)) for step in range(1, ALONG_X)
    ]
    for copy in x_copies:
        copy.wait_recv()
    rz[z] = jnp.sum(rx[...], axis=0)
    z_copies = [
        send(rz.at[z], rz.at[z], s_send.at[9 + step], s_recv.at[9 + step], z_at(step)) for step in range(1, rows_z)
    ]
    for copy in z_copies:
        copy.wait_recv()
    gram_out[...] = jnp.sum(rz[...], axis=0) * (1.0 / (domains * 32768))

    for copy in v_copies + q_copies + s_copies + x_copies + z_copies:
        copy.wait_send()
    for copies in h_copies + w_copies:
        for copy in copies:
            copy.wait_send()


def local(domains, bands, orbitals, potential, coupling, projectors, slot_atom, slot_domain_block, slot_count):
    vmem = pl.BlockSpec(memory_space=pltpu.VMEM)
    smem = pl.BlockSpec(memory_space=pltpu.SMEM)
    shift = domains // ALONG_X + ALONG_X + bands - 3
    return pl.pallas_call(
        functools.partial(kernel, domains, bands),
        out_shape=(
            jax.ShapeDtypeStruct((16, 8, 32, 128), BF16),
            jax.ShapeDtypeStruct((16, 128), F32),
        ),
        in_specs=[vmem, vmem, smem, vmem, vmem, vmem, smem],
        out_specs=(vmem, vmem),
        scratch_shapes=[
            pltpu.VMEM((8, 16, 4096), BF16),
            pltpu.VMEM((8, 16, 4096), BF16),
            pltpu.VMEM((8, 16, 4096), BF16),
            pltpu.VMEM((8, 16, 4096), BF16),
            pltpu.VMEM((4, 16, 32, 128), BF16),
            pltpu.VMEM((4, 16, 32, 128), BF16),
            pltpu.VMEM((16, 8, 32, 128), F32),
            pltpu.VMEM((256, 256), BF16),
            pltpu.VMEM((256, 256), BF16),
            pltpu.VMEM((256, 128), F32),
            pltpu.VMEM((192, 256), BF16),
            pltpu.VMEM((8, 64, 256), F32),
            pltpu.VMEM((8, 16, 256), F32),
            pltpu.VMEM((8, 16, 256), F32),
            pltpu.VMEM((3, 64, 128), F32),
            pltpu.VMEM((6, 64, 128), F32),
            pltpu.VMEM((256, 256), BF16),
            pltpu.VMEM((512, 256), BF16),
            pltpu.VMEM((128, 256), BF16),
            pltpu.VMEM((128, 128), F32),
            pltpu.VMEM((8, 16, 128), F32),
            pltpu.VMEM((ALONG_X, 16, 128), F32),
            pltpu.VMEM((domains // ALONG_X, 16, 128), F32),
            pltpu.SemaphoreType.DMA,
            pltpu.SemaphoreType.DMA((7,)),
            pltpu.SemaphoreType.DMA((7,)),
            pltpu.SemaphoreType.DMA((4, 7)),
            pltpu.SemaphoreType.DMA((4, 7)),
            pltpu.SemaphoreType.DMA((2, 4)),
            pltpu.SemaphoreType.DMA((2, 4)),
            pltpu.SemaphoreType.DMA((4,)),
            pltpu.SemaphoreType.DMA((4,)),
            pltpu.SemaphoreType.DMA((shift,)),
            pltpu.SemaphoreType.DMA((shift,)),
            pltpu.SemaphoreType.DMA((1,)),
        ],
        compiler_params=pltpu.CompilerParams(
            collective_id=0, has_side_effects=True, vmem_limit_bytes=40 * 1024 * 1024
        ),
    )(
        orbitals, potential, coupling, projectors,
        slot_atom.reshape(1, -1), slot_domain_block.reshape(1, -1), slot_count,
    )


def solution(mesh):
    return jax.shard_map(
        functools.partial(local, mesh.shape["dom"], mesh.shape["band"]),
        mesh=mesh,
        in_specs=(
            P("band", "dom", None, None),
            P("dom", None, None),
            P(),
            P("dom", None),
            P("dom"),
            P("dom"),
            P("dom"),
        ),
        out_specs=(P("band", "dom", None, None), P("band", None)),
        check_vma=False,
    )
```

time: 346 us -> 64.5 us (0.19)
  the two profiles are of different devices: /device:TPU:0 before, /device:TPU:6 now
where the time goes in v1:
time: 64.5 us; the launch traced here: 64.3 us
  Pallas kernels  57 us (88%)
  local copies, waits for them, and re-layouts  6 us (9%)
  between operations  1.32 us (2%)
    pallas_call x1, Pallas kernels, local(): pl.pallas_call(functools.partial(kernel, domains, bands), out_shape=(jax....  57 us
    unnamed x14, local copies, waits for them, and re-layouts  6 us

profile of v1, /device:TPU:6, one launch (start us, length us, event | category | flops | bytes accessed | tf_op | source)
XLA Modules:
  0.0 64.3 jit_solution(16403547241550714406)
XLA Ops:
  0.6 0.0 copy-start.3
  1.3 0.0 copy-start.4
  1.3 0.0 copy-done.3
  1.3 0.7 %copy-done.4 = s32[256]{0:T(256)S(1)} copy-done((s32[256]{0:T(256)S(1)}, s32[256]{0:T(256)}, u32[]{:S(2)}) %copy-start.4) | copy-done | bytes 1048
  2.0 0.0 copy-start
  2.0 1.2 %copy-done = bf16[16,8,32,128]{3,2,1,0:T(8,128)(2,1)S(1)} copy-done((bf16[16,8,32,128]{3,2,1,0:T(8,128)(2,1)S(1)}, bf16[16,8,32,128]{3,2,1,0:T(8,128)(2,1)}, u32[]{:S(2)}) %copy-start) | copy-done | bytes 1048600
  3.2 0.0 copy-start.1
  3.2 0.9 %copy-done.1 = bf16[256,512]{1,0:T(8,128)(2,1)S(1)} copy-done((bf16[256,512]{1,0:T(8,128)(2,1)S(1)}, bf16[256,512]{1,0:T(8,128)(2,1)}, u32[]{:S(2)}) %copy-start.1) | copy-done | bytes 262168
  4.2 0.0 copy-start.2
  4.2 0.9 %copy-done.2 = f32[8,32,128]{2,1,0:T(8,128)S(1)} copy-done((f32[8,32,128]{2,1,0:T(8,128)S(1)}, f32[8,32,128]{2,1,0:T(8,128)}, u32[]{:S(2)}) %copy-start.2) | copy-done | bytes 131096
  5.1 0.0 copy-start.5
  5.1 0.7 %copy-done.5 = s32[256]{0:T(256)S(1)} copy-done((s32[256]{0:T(256)S(1)}, s32[256]{0:T(256)}, u32[]{:S(2)}) %copy-start.5) | copy-done | bytes 1048
  5.7 57.0 %shard_map.86 = (bf16[16,8,32,128]{3,2,1,0:T(8,128)(2,1)S(1)}, f32[16,128]{1,0:T(8,128)S(1)}) custom-call(bf16[16,8,32,128]{3,2,1,0:T(8,128)(2,1)S(1)} %copy-done, f32[8,32,128]{2,1,0:T(8,128)S(1)} %copy-done.2, f32[8,8]{1,0:T(8,128)S(1)} %copy-done.3, bf16[256,512]{1,0:T(8,128)(2,1)S(1)} %copy-done.1, s32[1,256]{1,0:T(1,128)S(1)} %bitcast.2, ...), custom_call_target="tpu_custom_call" | custom-call | tf_op jit(solution)/shard_map/pallas_call | solution.py:261
  62.7 1.0 %copy.12 = bf16[16,8,32,128]{3,2,1,0:T(8,128)(2,1)} copy(bf16[16,8,32,128]{3,2,1,0:T(8,128)(2,1)S(1)} %get-tuple-element.4) | data formatting | bytes 2097152
  63.7 0.6 copy.13
Async XLA Ops:
  0.6 0.7 %copy-start.3 = (f32[8,8]{1,0:T(8,128)S(1)}, f32[8,8]{1,0:T(8,128)}, u32[]{:S(2)}) copy-start(f32[8,8]{1,0:T(8,128)} %coupling.1) | copy-start | bytes 772
  1.3 0.7 %copy-start.4 = (s32[256]{0:T(256)S(1)}, s32[256]{0:T(256)}, u32[]{:S(2)}) copy-start(s32[256]{0:T(256)} %param.11) | copy-start | bytes 3076
  2.0 1.2 %copy-start = (bf16[16,8,32,128]{3,2,1,0:T(8,128)(2,1)S(1)}, bf16[16,8,32,128]{3,2,1,0:T(8,128)(2,1)}, u32[]{:S(2)}) copy-start(bf16[16,8,32,128]{3,2,1,0:T(8,128)(2,1)} %v.1) | copy-start | bytes 3145732
  3.2 0.9 %copy-start.1 = (bf16[256,512]{1,0:T(8,128)(2,1)S(1)}, bf16[256,512]{1,0:T(8,128)(2,1)}, u32[]{:S(2)}) copy-start(bf16[256,512]{1,0:T(8,128)(2,1)} %proj.1) | copy-start | bytes 786436
  4.2 0.9 %copy-start.2 = (f32[8,32,128]{2,1,0:T(8,128)S(1)}, f32[8,32,128]{2,1,0:T(8,128)}, u32[]{:S(2)}) copy-start(f32[8,32,128]{2,1,0:T(8,128)} %pot.1) | copy-start | bytes 393220
  5.1 0.7 %copy-start.5 = (s32[256]{0:T(256)S(1)}, s32[256]{0:T(256)}, u32[]{:S(2)}) copy-start(s32[256]{0:T(256)} %param.12) | copy-start | bytes 3076

commit v2 on v1

v2 whole, which is shorter than its diff:
```python
import functools

import jax
import jax.numpy as jnp
from jax import lax
from jax.experimental import pallas as pl
from jax.experimental.pallas import tpu as pltpu
from jax.sharding import PartitionSpec as P

MESH = pl.DeviceIdType.MESH
F32 = jnp.float32
BF16 = jnp.bfloat16
STENCIL = (-205.0 / 72.0, 8.0 / 5.0, -1.0 / 5.0, 8.0 / 315.0, -1.0 / 560.0)
NN = (((1,), (0,)), ((), ()))
NT = (((1,), (1,)), ((), ()))
LANES = 16
REACH = 4


def mm(a, b, dims=NN):
    return lax.dot_general(a, b, dims, preferred_element_type=F32)


def iota(shape, dim):
    return lax.broadcasted_iota(jnp.int32, shape, dim)


def one(mask):
    return jnp.where(mask, 1.0, 0.0).astype(BF16)


def split(value):
    high = value.astype(BF16)
    return high, (value - high.astype(F32)).astype(BF16)


def plane_matrix():
    r, c = iota((256, 256), 0), iota((256, 256), 1)
    same_plane, same_row = (r >> 5) == (c >> 5), (r & 31) == (c & 31)
    apart, turn = jnp.abs((r >> 5) - (c >> 5)), ((r & 31) - (c & 31)) & 31
    value = jnp.where(r == c, -1.5 * STENCIL[0], 0.0)
    for k in range(1, 5):
        value = jnp.where(same_plane & ((turn == k) | (turn == 32 - k)), -0.5 * STENCIL[k], value)
        value = jnp.where(same_row & (apart == k), -0.5 * STENCIL[k], value)
    return value


def lane_matrix():
    turn = (iota((128, 128), 0) - iota((128, 128), 1)) & 127
    value = jnp.zeros((128, 128), F32)
    for k in range(1, 5):
        value = jnp.where((turn == k) | (turn == 128 - k), -0.5 * STENCIL[k], value)
    return value


def boundary_matrix(parity):
    r, c = iota((128, 128), 0), iota((128, 128), 1)
    apart = ((c >> 5) - (r >> 5)) * (1 - 2 * parity)
    value = jnp.zeros((128, 128), F32)
    for k in range(1, 5):
        value = jnp.where(((r & 31) == (c & 31)) & (apart == 4 - k), -0.5 * STENCIL[k], value)
    return value


def kernel(
    domains, bands,
    v_in, pot_in, coupling, proj_in, atom_in, block_in, count,
    out, gram_out,
    v, pot, proj, atom, block, tv, vt, va, hb, low, high, acc, gt, at, pt, cf, sp, q, rq, pm, lm, zm, mb, pott, p3, ra,
    gram, rb, rd,
    in_sem, a_send, a_recv, b_send, b_recv, f_send, f_recv, h_send, h_recv, q_send, q_recv, n_send, n_recv, s_send, s_recv, own_sem,
):
    dom, band = lax.axis_index("dom"), lax.axis_index("band")

    def dom_at(step):
        return {"dom": lax.rem(dom + step + domains, domains)}

    def band_at(step):
        return {"band": lax.rem(band + step, bands)}

    loads = [
        pltpu.make_async_copy(src, dst, in_sem.at[place])
        for place, (src, dst) in enumerate(
            ((v_in, v), (block_in, block), (proj_in, proj), (atom_in, atom), (pot_in, pot))
        )
    ]
    for load in loads:
        load.start()

    peers = [band_at(step) for step in range(1, bands)] + [dom_at(step) for step in range(1, domains)]
    barrier = pltpu.get_barrier_semaphore()
    for peer in peers:
        pl.semaphore_signal(barrier, inc=1, device_id=peer, device_id_type=MESH)

    def send(src, dst, send_sem, recv_sem, peer):
        copy = pltpu.make_async_remote_copy(
            src_ref=src, dst_ref=dst, send_sem=send_sem, recv_sem=recv_sem, device_id=peer, device_id_type=MESH
        )
        copy.start()
        return copy

    r, c = iota((256, 256), 0), iota((256, 256), 1)
    loads[0].wait()
    pm[...] = one(((r & 15) == (c >> 4)) & ((r >> 4) == (c & 15)))

    small_eye = one(iota((128, 128), 0) == iota((128, 128), 1))

    @pl.loop(0, 16, step=4)
    def _(first):
        for i in range(4):
            tv[first + i] = mm(small_eye, v[first + i].reshape(256, 128), NT).astype(BF16)

    for share in range(8):
        span = slice(LANES * share, LANES * share + LANES)
        tiles = mm(pm[...], tv[:, span, :].reshape(256, 256)).astype(BF16).reshape(LANES, 16, 256)
        vt[0, span] = tiles[:, :, 0:128]
        vt[1, span] = tiles[:, :, 128:256]
    vt[:, 128 : 128 + REACH] = vt[:, 0:REACH]

    pl.semaphore_wait(barrier, len(peers))

    parity = lax.rem(band, 2)
    a_copies, b_copies = [], []
    for step in range(1, bands):
        peer = band_at(step)
        other, side = peer["band"], lax.rem(peer["band"], 2)
        a_copies.append(send(
            vt.at[side, pl.ds(LANES * other, LANES)], va.at[band, side, pl.ds(0, LANES)],
            a_send.at[step - 1], a_recv.at[step - 1], peer,
        ))
    own = pltpu.make_async_copy(vt.at[:, pl.ds(LANES * band, LANES + REACH)], va.at[band], own_sem.at[0])
    own.start()

    def send_halos(k):
        return (
            send(v.at[:, 8 - k], low.at[4 - k], h_send.at[0, k - 1], h_recv.at[0, k - 1], dom_at(1)),
            send(v.at[:, k - 1], high.at[k - 1], h_send.at[1, k - 1], h_recv.at[1, k - 1], dom_at(-1)),
        )

    h_copies = [send_halos(1), send_halos(2)]
    for step in range(1, bands):
        peer = band_at(step)
        other, side = peer["band"], lax.rem(peer["band"], 2)
        b_copies.append(send(
            vt.at[1 - side, pl.ds(LANES * other, LANES + REACH)], va.at[band, 1 - side],
            b_send.at[0, step - 1], b_recv.at[0, step - 1], peer,
        ))
        b_copies.append(send(
            vt.at[side, pl.ds(LANES * other + LANES, REACH)], va.at[band, side, pl.ds(LANES, REACH)],
            b_send.at[1, step - 1], b_recv.at[1, step - 1], peer,
        ))

    onward = dom_at(2 * parity - 1)

    def forward(source, place):
        return send(va.at[source, parity, pl.ds(0, LANES)], hb.at[source], f_send.at[place], f_recv.at[place], onward)

    for load in loads[1:]:
        load.wait()
    half_of = block[...] & 1
    live = iota((1, 256), 1) < count[0]
    gt[...] = one((r == (block[...] >> 1)) & live)
    window = (((atom[...] >> 6) - dom + 1 + domains) & (domains - 1)) * 64 + (atom[...] & 63)
    at[...] = one(iota((192, 256), 0) == window)
    for pair in range(4):
        pt[2 * pair : 2 * pair + 2] = mm(small_eye, proj[:, 128 * pair : 128 * pair + 128], NT).reshape(2, 64, 256)

    @pl.loop(0, 16, step=4)
    def _(first):
        picked = mm(tv[pl.ds(first, 4)].reshape(512, 256), gt[...])
        for i in range(4):
            points = jnp.where(half_of == 0, picked[128 * i : 128 * i + 64], picked[128 * i + 64 : 128 * i + 128])
            for p in range(8):
                cf[p, pl.ds(first + i, 1), :] = jnp.sum(points * pt[p], axis=0, keepdims=True)

    rest = cf[...].reshape(128, 256)
    total = jnp.zeros((192, 128), F32)
    for _ in range(3):
        part = rest.astype(BF16)
        rest = rest - part.astype(F32)
        total = total + mm(at[...], part, NT)
    q[...] = total.reshape(3, 64, 128)
    q_copies = [
        send(q.at[pl.ds(1, 2)], rq.at[pl.ds(1, 2)], q_send.at[0], q_recv.at[0], dom_at(1)),
        send(q.at[pl.ds(0, 2)], rq.at[pl.ds(3, 2)], q_send.at[1], q_recv.at[1], dom_at(-1)),
        send(q.at[2], rq.at[0], q_send.at[2], q_recv.at[2], dom_at(2)),
        send(q.at[0], rq.at[5], q_send.at[3], q_recv.at[3], dom_at(-2)),
    ]

    lm[:, 0:256], lm[:, 256:512] = split(plane_matrix())
    zm[0:128], zm[128:256] = split(lane_matrix())

    @pl.loop(0, 16, step=2)
    def _(first):
        values = [v[first + i].reshape(256, 128) for i in range(2)]
        wide = jnp.concatenate(values, axis=1)
        summed = mm(lm[...], jnp.concatenate([wide, wide], axis=0))
        for i in range(2):
            lanes = mm(jnp.concatenate([values[i], values[i]], axis=1), zm[...])
            local_part = summed[:, 128 * i : 128 * i + 128] + lanes + pot[...].reshape(256, 128) * values[i].astype(F32)
            acc[first + i] = local_part.reshape(8, 32, 128)

    rows = []
    for p in range(8):
        line = jnp.zeros((16, 128), F32)
        for j in range(8):
            line = jnp.where((iota((16, 128), 1) >> 4) == j, coupling[p, j], line)
        rows.append(jnp.where((iota((16, 128), 1) & 15) == iota((16, 128), 0), line, 0.0))
    mixing = jnp.concatenate(rows, axis=0)

    for copy in q_copies:
        copy.wait_recv()
    owned = jnp.concatenate([rq[0] + rq[1] + q[0], rq[2] + q[1] + rq[3], q[2] + rq[4] + rq[5]], axis=0)
    coupled = lax.dot_general(mixing, owned, NT, precision=lax.Precision.HIGHEST, preferred_element_type=F32)
    own_rows = owned[64:128]
    p3[:, 0:128] = mm(small_eye, jnp.concatenate(split(own_rows), axis=0), NT).astype(BF16)
    p3[:, 128:256] = lax.dot_general(
        mixing, jnp.concatenate([own_rows, own_rows], axis=0), NT, precision=lax.Precision.HIGHEST, preferred_element_type=F32
    ).astype(BF16)
    n_copies = []
    for step in range(1, bands):
        peer = band_at(step)
        n_copies.append(send(
            p3.at[pl.ds(pl.multiple_of(peer["band"] * 16, 16), 16)], ra.at[band],
            n_send.at[step - 1], n_recv.at[step - 1], peer,
        ))
    ra[band] = p3[pl.ds(pl.multiple_of(band * 16, 16), 16), :]
    sp[...] = mm(coupled.astype(BF16), at[...]).reshape(8, 16, 256)

    gt_twice = jnp.concatenate([gt[...], gt[...]], axis=1)

    @pl.loop(0, 16, step=2)
    def _(first):
        placed = []
        for i in range(2):
            added = pt[0] * sp[0, pl.ds(first + i, 1), :]
            for p in range(1, 8):
                added = added + pt[p] * sp[p, pl.ds(first + i, 1), :]
            placed += [jnp.where(half_of == 0, added, 0.0), jnp.where(half_of == 1, added, 0.0)]
        parts = split(jnp.concatenate(placed, axis=0))
        projected = mm(gt_twice, jnp.concatenate(parts, axis=1), NT)
        for i in range(2):
            acc[first + i] = acc[first + i] + projected[:, 128 * i : 128 * i + 128].reshape(8, 32, 128)

    own.wait()
    f_copies = [forward(band, 0)]
    for step, copy in enumerate(a_copies, 1):
        copy.wait_recv()
        f_copies.append(forward(lax.rem(band - step + bands, bands), step))
    h_copies += [send_halos(3), send_halos(4)]

    def finish(k):
        for copy in h_copies[k - 1]:
            copy.wait_recv()
        for side in range(2):
            plane = 3 + k if side else 4 - k
            for half in range(2):
                span = slice(16 * half, 16 * half + 16)
                value = acc[:, plane, span, :]
                for near in range(k):
                    halo = high[near, :, span, :] if side else low[3 - near, :, span, :]
                    reach = 8 + near - plane if side else plane + 1 + near
                    value = value - 0.5 * STENCIL[reach] * halo.astype(F32)
                out[:, plane, span, :] = value.astype(BF16)

    finish(1)
    finish(2)

    pott[...] = pot[...].reshape(256, 128).T
    mb[0:128], mb[128:256] = split(boundary_matrix(parity))
    gram[...] = jnp.zeros_like(gram)
    for copy in b_copies:
        copy.wait_recv()

    @pl.loop(0, LANES, step=4)
    def _(first):
        lanes = [
            jnp.concatenate([va[:, 0, first + i].reshape(128, 128), va[:, 1, first + i].reshape(128, 128)], axis=1)
            for i in range(8)
        ]
        images = []
        for i in range(4):
            weights = pott[pl.ds(LANES * band + first + i, 1), :]
            image = mm(jnp.concatenate([lanes[i], lanes[i]], axis=1), lm[...], NT) + weights * lanes[i].astype(F32)
            images.append(image.astype(BF16))
        rows = [jnp.concatenate(images, axis=1)]
        rows += [jnp.concatenate(lanes[k : k + 4], axis=1) for k in range(1, 5)]
        gram[:, 0:640] += mm(jnp.concatenate(lanes[0:4], axis=1), jnp.concatenate(rows, axis=0), NT)

    for copy in f_copies:
        copy.wait_recv()

    @pl.loop(0, LANES, step=4)
    def _(first):
        near, far = [], []
        for i in range(4):
            near.append(va[:, 1 - parity, first + i].reshape(128, 128))
            across = hb[:, first + i].reshape(128, 128)
            far.append(mm(jnp.concatenate([across, across], axis=1), mb[...]).astype(BF16))
        gram[:, 640:768] += mm(jnp.concatenate(near, axis=1), jnp.concatenate(far, axis=1), NT)

    for copy in n_copies:
        copy.wait_recv()
    once = gram[:, 640:768]
    for k in range(1, 5):
        once = once - 0.5 * STENCIL[k] * gram[:, 128 * k : 128 * k + 128]
    nonlocal_part = mm(ra[:, :, 0:128].reshape(128, 128), ra[:, :, 128:256].reshape(128, 128), NT)
    gram[:, 0:128] = gram[:, 0:128] + once + once.T + nonlocal_part

    s_copies = []
    for step in range(1, bands):
        peer = band_at(step)
        s_copies.append(send(
            gram.at[pl.ds(pl.multiple_of(peer["band"] * 16, 16), 16), pl.ds(0, 128)], rb.at[band],
            s_send.at[step - 1], s_recv.at[step - 1], peer,
        ))
    rb[band] = gram[pl.ds(pl.multiple_of(band * 16, 16), 16), 0:128]
    finish(3)
    for copy in s_copies:
        copy.wait_recv()
    rd[dom] = jnp.sum(rb[...], axis=0)
    d_copies = [
        send(rd.at[dom], rd.at[dom], s_send.at[bands - 2 + step], s_recv.at[bands - 2 + step], dom_at(step))
        for step in range(1, domains)
    ]
    finish(4)
    for copy in d_copies:
        copy.wait_recv()
    gram_out[...] = jnp.sum(rd[...], axis=0) * (1.0 / (domains * 32768))

    for copy in a_copies + b_copies + f_copies + q_copies + n_copies + s_copies + d_copies:
        copy.wait_send()
    for copies in h_copies:
        for copy in copies:
            copy.wait_send()


def local(domains, bands, orbitals, potential, coupling, projectors, slot_atom, slot_domain_block, slot_count):
    vmem = pl.BlockSpec(memory_space=pltpu.VMEM)
    smem = pl.BlockSpec(memory_space=pltpu.SMEM)
    hbm = pl.BlockSpec(memory_space=pltpu.HBM)
    sums = bands + domains - 2
    return pl.pallas_call(
        functools.partial(kernel, domains, bands),
        out_shape=(
            jax.ShapeDtypeStruct((16, 8, 32, 128), BF16),
            jax.ShapeDtypeStruct((16, 128), F32),
        ),
        in_specs=[hbm, hbm, smem, hbm, hbm, hbm, smem],
        out_specs=(vmem, vmem),
        scratch_shapes=[
            pltpu.VMEM((16, 8, 32, 128), BF16),
            pltpu.VMEM((8, 32, 128), F32),
            pltpu.VMEM((256, 512), BF16),
            pltpu.VMEM((1, 256), jnp.int32),
            pltpu.VMEM((1, 256), jnp.int32),
            pltpu.VMEM((16, 128, 256), BF16),
            pltpu.VMEM((2, 128 + REACH, 16, 128), BF16),
            pltpu.VMEM((8, 2, LANES + REACH, 16, 128), BF16),
            pltpu.VMEM((8, LANES, 16, 128), BF16),
            pltpu.VMEM((4, 16, 32, 128), BF16),
            pltpu.VMEM((4, 16, 32, 128), BF16),
            pltpu.VMEM((16, 8, 32, 128), F32),
            pltpu.VMEM((256, 256), BF16),
            pltpu.VMEM((192, 256), BF16),
            pltpu.VMEM((8, 64, 256), F32),
            pltpu.VMEM((8, 16, 256), F32),
            pltpu.VMEM((8, 16, 256), F32),
            pltpu.VMEM((3, 64, 128), F32),
            pltpu.VMEM((6, 64, 128), F32),
            pltpu.VMEM((256, 256), BF16),
            pltpu.VMEM((256, 512), BF16),
            pltpu.VMEM((256, 128), BF16),
            pltpu.VMEM((256, 128), BF16),
            pltpu.VMEM((128, 256), F32),
            pltpu.VMEM((128, 256), BF16),
            pltpu.VMEM((8, 16, 256), BF16),
            pltpu.VMEM((128, 768), F32),
            pltpu.VMEM((8, 16, 128), F32),
            pltpu.VMEM((domains, 16, 128), F32),
            pltpu.SemaphoreType.DMA((5,)),
            pltpu.SemaphoreType.DMA((7,)),
            pltpu.SemaphoreType.DMA((7,)),
            pltpu.SemaphoreType.DMA((2, 7)),
            pltpu.SemaphoreType.DMA((2, 7)),
            pltpu.SemaphoreType.DMA((8,)),
            pltpu.SemaphoreType.DMA((8,)),
            pltpu.SemaphoreType.DMA((2, 4)),
            pltpu.SemaphoreType.DMA((2, 4)),
            pltpu.SemaphoreType.DMA((4,)),
            pltpu.SemaphoreType.DMA((4,)),
            pltpu.SemaphoreType.DMA((7,)),
            pltpu.SemaphoreType.DMA((7,)),
            pltpu.SemaphoreType.DMA((sums,)),
            pltpu.SemaphoreType.DMA((sums,)),
            pltpu.SemaphoreType.DMA((1,)),
        ],
        compiler_params=pltpu.CompilerParams(
            collective_id=0, has_side_effects=True, vmem_limit_bytes=62 * 1024 * 1024
        ),
    )(
        orbitals, potential, coupling, projectors,
        slot_atom.reshape(1, -1), slot_domain_block.reshape(1, -1), slot_count,
    )


def solution(mesh):
    return jax.shard_map(
        functools.partial(local, mesh.shape["dom"], mesh.shape["band"]),
        mesh=mesh,
        in_specs=(
            P("band", "dom", None, None),
            P("dom", None, None),
            P(),
            P("dom", None),
            P("dom"),
            P("dom"),
            P("dom"),
        ),
        out_specs=(P("band", "dom", None, None), P("band", None)),
        check_vma=False,
    )
```

time: 64.5 us -> 58 us (0.90)
  Pallas kernels: 57 us -> 53.6 us
  local copies, waits for them, and re-layouts: 6 us -> 2.9 us
    pallas_call x1, Pallas kernels: 57 us -> 53.6 us  [local(): pl.pallas_call(functools.partial(kernel, domains, bands), out_shape=(jax....]
    unnamed x14 -> x4, local copies, waits for them, and re-layouts: 6 us -> 2.9 us
where the time goes in v2:
time: 58 us; the launch traced here: 57.8 us
  Pallas kernels  53.6 us (92%)
  local copies, waits for them, and re-layouts  2.9 us (5%)
  between operations  1.3 us (2%)
    pallas_call x1, Pallas kernels, local(): pl.pallas_call(functools.partial(kernel, domains, bands), out_shape=(jax....  53.6 us
    unnamed x4, local copies, waits for them, and re-layouts  2.9 us

profile of v2, /device:TPU:6, one launch (start us, length us, event | category | flops | bytes accessed | tf_op | source)
XLA Modules:
  0.0 57.8 jit_solution(2020988781780134089)
XLA Ops:
  1.3 53.6 %shard_map.86 = (bf16[16,8,32,128]{3,2,1,0:T(8,128)(2,1)}, f32[16,128]{1,0:T(8,128)}) custom-call(bf16[16,8,32,128]{3,2,1,0:T(8,128)(2,1)} %v_in.1, f32[8,32,128]{2,1,0:T(8,128)} %pot_in.1, f32[8,8]{1,0:T(8,128)} %coupling.1, bf16[256,512]{1,0:T(8,128)(2,1)} %proj_in.1, s32[1,256]{1,0:T(1,128)} %bitcast.2, s32[1,256]{1,0:T(1,128)} %bitcast.3, s32[1]{0:T(128)S(6)} %copy.11.count), custom_call_target="tpu_custom_call" | custom-call | tf_op jit(solution)/shard_map/pallas_call | solution.py:343
  54.9 0.0 copy-start
  54.9 2.3 %copy.12 = bf16[16,8,32,128]{3,2,1,0:T(8,128)(2,1)} copy(bf16[16,8,32,128]{3,2,1,0:T(8,128)(2,1)} %get-tuple-element.4) | data formatting | bytes 2097152
  57.2 0.0 copy-done
  57.2 0.6 %copy.13 = f32[16,128]{1,0:T(8,128)} copy(f32[16,128]{1,0:T(8,128)S(1)} %copy-done) | data formatting | bytes 16384
Async XLA Ops:
  54.9 2.3 %copy-start = (f32[16,128]{1,0:T(8,128)S(1)}, f32[16,128]{1,0:T(8,128)}, u32[]{:S(2)}) copy-start(f32[16,128]{1,0:T(8,128)} %get-tuple-element.5) | copy-start | bytes 24580

commit v3 on v2

--- a/solution.py
+++ b/solution.py
@@ -65,8 +65,8 @@
 def kernel(
     domains, bands,
     v_in, pot_in, coupling, proj_in, atom_in, block_in, count,
-    out, gram_out,
-    v, pot, proj, atom, block, tv, vt, va, hb, low, high, acc, gt, at, pt, cf, sp, q, rq, pm, lm, zm, mb, pott, p3, ra,
+    out_hbm, gram_out,
+    out, v, pot, proj, atom, block, tv, vt, va, hb, low, high, acc, gt, at, pt, cf, sp, q, rq, pm, lm, zm, mb, pott, p3, ra,
     gram, rb, rd,
     in_sem, a_send, a_recv, b_send, b_recv, f_send, f_recv, h_send, h_recv, q_send, q_recv, n_send, n_recv, s_send, s_recv, own_sem,
 ):
@@ -81,10 +81,14 @@
     loads = [
         pltpu.make_async_copy(src, dst, in_sem.at[place])
         for place, (src, dst) in enumerate(
-            ((v_in, v), (block_in, block), (proj_in, proj), (atom_in, atom), (pot_in, pot))
+            ((block_in, block), (proj_in, proj), (atom_in, atom), (pot_in, pot))
         )
     ]
-    for load in loads:
+    v_loads = [
+        pltpu.make_async_copy(v_in.at[pl.ds(4 * part, 4)], v.at[pl.ds(4 * part, 4)], in_sem.at[4 + part])
+        for part in range(4)
+    ]
+    for load in v_loads + loads:
         load.start()
 
     peers = [band_at(step) for step in range(1, bands)] + [dom_at(step) for step in range(1, domains)]
@@ -100,15 +104,14 @@
         return copy
 
     r, c = iota((256, 256), 0), iota((256, 256), 1)
-    loads[0].wait()
     pm[...] = one(((r & 15) == (c >> 4)) & ((r >> 4) == (c & 15)))
 
     small_eye = one(iota((128, 128), 0) == iota((128, 128), 1))
 
-    @pl.loop(0, 16, step=4)
-    def _(first):
-        for i in range(4):
-            tv[first + i] = mm(small_eye, v[first + i].reshape(256, 128), NT).astype(BF16)
+    for part in range(4):
+        v_loads[part].wait()
+        for o in range(4 * part, 4 * part + 4):
+            tv[o] = mm(small_eye, v[o].reshape(256, 128), NT).astype(BF16)
 
     for share in range(8):
         span = slice(LANES * share, LANES * share + LANES)
@@ -155,7 +158,7 @@
     def forward(source, place):
         return send(va.at[source, parity, pl.ds(0, LANES)], hb.at[source], f_send.at[place], f_recv.at[place], onward)
 
-    for load in loads[1:]:
+    for load in loads:
         load.wait()
     half_of = block[...] & 1
     live = iota((1, 256), 1) < count[0]
@@ -187,6 +190,11 @@
         send(q.at[0], rq.at[5], q_send.at[3], q_recv.at[3], dom_at(-2)),
     ]
 
+    own.wait()
+    f_copies = [forward(band, 0)]
+    for step, copy in enumerate(a_copies, 1):
+        copy.wait_recv()
+        f_copies.append(forward(lax.rem(band - step + bands, bands), step))
     lm[:, 0:256], lm[:, 256:512] = split(plane_matrix())
     zm[0:128], zm[128:256] = split(lane_matrix())
 
@@ -242,12 +250,6 @@
         for i in range(2):
             acc[first + i] = acc[first + i] + projected[:, 128 * i : 128 * i + 128].reshape(8, 32, 128)
 
-    own.wait()
-    f_copies = [forward(band, 0)]
-    for step, copy in enumerate(a_copies, 1):
-        copy.wait_recv()
-        f_copies.append(forward(lax.rem(band - step + bands, bands), step))
-    h_copies += [send_halos(3), send_halos(4)]
 
     def finish(k):
         for copy in h_copies[k - 1]:
@@ -271,6 +273,7 @@
     gram[...] = jnp.zeros_like(gram)
     for copy in b_copies:
         copy.wait_recv()
+    h_copies += [send_halos(3), send_halos(4)]
 
     @pl.loop(0, LANES, step=4)
     def _(first):
@@ -318,16 +321,19 @@
     finish(3)
     for copy in s_copies:
         copy.wait_recv()
-    rd[dom] = jnp.sum(rb[...], axis=0)
+    rd[dom] = jnp.sum(rb[...], axis=0).astype(BF16)
     d_copies = [
         send(rd.at[dom], rd.at[dom], s_send.at[bands - 2 + step], s_recv.at[bands - 2 + step], dom_at(step))
         for step in range(1, domains)
     ]
     finish(4)
+    leave = pltpu.make_async_copy(out, out_hbm, own_sem.at[1])
+    leave.start()
     for copy in d_copies:
         copy.wait_recv()
-    gram_out[...] = jnp.sum(rd[...], axis=0) * (1.0 / (domains * 32768))
-
+    gram_out[...] = jnp.sum(rd[...].astype(F32), axis=0) * (1.0 / (domains * 32768))
+
+    leave.wait()
     for copy in a_copies + b_copies + f_copies + q_copies + n_copies + s_copies + d_copies:
         copy.wait_send()
     for copies in h_copies:
@@ -335,20 +341,40 @@
             copy.wait_send()
 
 
+PARTS = 4
+
+
+def place(applied, gram, applied_out, gram_out, held, held_gram, come, go):
+    refs = [
+        (applied.at[pl.ds(16 // PARTS * part, 16 // PARTS)], held.at[pl.ds(16 // PARTS * part, 16 // PARTS)],
+         applied_out.at[pl.ds(16 // PARTS * part, 16 // PARTS)])
+        for part in range(PARTS)
+    ]
+    refs.append((gram, held_gram, gram_out))
+    arriving = [pltpu.make_async_copy(src, held_part, come.at[i]) for i, (src, held_part, _) in enumerate(refs)]
+    leaving = [pltpu.make_async_copy(held_part, dst, go.at[i]) for i, (_, held_part, dst) in enumerate(refs)]
+    for copy in arriving:
+        copy.start()
+    for first, second in zip(arriving, leaving):
+        first.wait()
+        second.start()
+    for copy in leaving:
+        copy.wait()
+
+
 def local(domains, bands, orbitals, potential, coupling, projectors, slot_atom, slot_domain_block, slot_count):
     vmem = pl.BlockSpec(memory_space=pltpu.VMEM)
     smem = pl.BlockSpec(memory_space=pltpu.SMEM)
     hbm = pl.BlockSpec(memory_space=pltpu.HBM)
     sums = bands + domains - 2
-    return pl.pallas_call(
+    shapes = (jax.ShapeDtypeStruct((16, 8, 32, 128), BF16), jax.ShapeDtypeStruct((16, 128), F32))
+    results = pl.pallas_call(
         functools.partial(kernel, domains, bands),
-        out_shape=(
-            jax.ShapeDtypeStruct((16, 8, 32, 128), BF16),
-            jax.ShapeDtypeStruct((16, 128), F32),
-        ),
+        out_shape=shapes,
         in_specs=[hbm, hbm, smem, hbm, hbm, hbm, smem],
-        out_specs=(vmem, vmem),
+        out_specs=(hbm, vmem),
         scratch_shapes=[
+            pltpu.VMEM((16, 8, 32, 128), BF16),
             pltpu.VMEM((16, 8, 32, 128), BF16),
             pltpu.VMEM((8, 32, 128), F32),
             pltpu.VMEM((256, 512), BF16),
@@ -377,8 +403,8 @@
             pltpu.VMEM((8, 16, 256), BF16),
             pltpu.VMEM((128, 768), F32),
             pltpu.VMEM((8, 16, 128), F32),
-            pltpu.VMEM((domains, 16, 128), F32),
-            pltpu.SemaphoreType.DMA((5,)),
+            pltpu.VMEM((domains, 16, 128), BF16),
+            pltpu.SemaphoreType.DMA((8,)),
             pltpu.SemaphoreType.DMA((7,)),
             pltpu.SemaphoreType.DMA((7,)),
             pltpu.SemaphoreType.DMA((2, 7)),
@@ -393,7 +419,7 @@
             pltpu.SemaphoreType.DMA((7,)),
             pltpu.SemaphoreType.DMA((sums,)),
             pltpu.SemaphoreType.DMA((sums,)),
-            pltpu.SemaphoreType.DMA((1,)),
+            pltpu.SemaphoreType.DMA((2,)),
         ],
         compiler_params=pltpu.CompilerParams(
             collective_id=0, has_side_effects=True, vmem_limit_bytes=62 * 1024 * 1024
@@ -402,6 +428,19 @@
         orbitals, potential, coupling, projectors,
         slot_atom.reshape(1, -1), slot_domain_block.reshape(1, -1), slot_count,
     )
+    return pl.pallas_call(
+        place,
+        out_shape=shapes,
+        in_specs=[hbm, hbm],
+        out_specs=(hbm, hbm),
+        scratch_shapes=[
+            pltpu.VMEM((16, 8, 32, 128), BF16),
+            pltpu.VMEM((16, 128), F32),
+            pltpu.SemaphoreType.DMA((PARTS + 1,)),
+            pltpu.SemaphoreType.DMA((PARTS + 1,)),
+        ],
+        compiler_params=pltpu.CompilerParams(vmem_limit_bytes=62 * 1024 * 1024),
+    )(*results)
 
 
 def solution(mesh):

time: 58 us -> 48.6 us (0.84)
  Pallas kernels: 53.6 us -> 47.1 us
  local copies, waits for them, and re-layouts: 2.9 us -> 0 us
    pallas_call x1 -> x2, Pallas kernels: 53.6 us -> 47.1 us  [the longest x1 45.1 us: local(): pl.pallas_call(functools.partial(kernel, domains, bands), out_shape=shape...]
    unnamed x4 -> x0, local copies, waits for them, and re-layouts: 2.9 us -> none
where the time goes in v3:
time: 48.6 us; the launch traced here: 48.4 us
  Pallas kernels  47.1 us (97%)
  between operations  1.29 us (3%)
    pallas_call x1, Pallas kernels, local(): pl.pallas_call(functools.partial(kernel, domains, bands), out_shape=shape...  45.1 us
    pallas_call x1, Pallas kernels, local(): pl.pallas_call(place, out_shape=shapes, in_specs=[hbm, hbm], out_specs=(h...  2 us

profile of v3, /device:TPU:6, one launch (start us, length us, event | category | flops | bytes accessed | tf_op | source)
XLA Modules:
  0.0 48.4 jit_solution(6739672378764782082)
XLA Ops:
  1.3 45.1 %shard_map.86 = (bf16[16,8,32,128]{3,2,1,0:T(8,128)(2,1)}, f32[16,128]{1,0:T(8,128)}) custom-call(bf16[16,8,32,128]{3,2,1,0:T(8,128)(2,1)} %v_in.1, f32[8,32,128]{2,1,0:T(8,128)} %pot_in.1, f32[8,8]{1,0:T(8,128)} %coupling.1, bf16[256,512]{1,0:T(8,128)(2,1)} %proj_in.1, s32[1,256]{1,0:T(1,128)} %bitcast.2, s32[1,256]{1,0:T(1,128)} %bitcast.3, s32[1]{0:T(128)S(6)} %copy.9.count), custom_call_target="tpu_custom_call" | custom-call | tf_op jit(solution)/shard_map/pallas_call | solution.py:371
  46.4 2.0 %shard_map.87 = (bf16[16,8,32,128]{3,2,1,0:T(8,128)(2,1)}, f32[16,128]{1,0:T(8,128)}) custom-call(bf16[16,8,32,128]{3,2,1,0:T(8,128)(2,1)} %get-tuple-element.4.applied, f32[16,128]{1,0:T(8,128)} %get-tuple-element.5.gram), custom_call_target="tpu_custom_call" | custom-call | tf_op jit(solution)/shard_map/pallas_call | solution.py:431

commit v4 on v3

--- a/solution.py
+++ b/solution.py
@@ -13,7 +13,8 @@
 STENCIL = (-205.0 / 72.0, 8.0 / 5.0, -1.0 / 5.0, 8.0 / 315.0, -1.0 / 560.0)
 NN = (((1,), (0,)), ((), ()))
 NT = (((1,), (1,)), ((), ()))
-LANES = 16
+LANES = 32
+HALF = 16
 REACH = 4
 
 
@@ -65,8 +66,8 @@
 def kernel(
     domains, bands,
     v_in, pot_in, coupling, proj_in, atom_in, block_in, count,
-    out_hbm, gram_out,
-    out, v, pot, proj, atom, block, tv, vt, va, hb, low, high, acc, gt, at, pt, cf, sp, q, rq, pm, lm, zm, mb, pott, p3, ra,
+    out, gram_out,
+    v, pot, proj, atom, block, tv, vt, va, hb, hc, low, high, acc, gt, at, pt, cf, sp, q, rq, pm, lm, zm, mb, pott, p3, ra,
     gram, rb, rd,
     in_sem, a_send, a_recv, b_send, b_recv, f_send, f_recv, h_send, h_recv, q_send, q_recv, n_send, n_recv, s_send, s_recv, own_sem,
 ):
@@ -91,7 +92,11 @@
     for load in v_loads + loads:
         load.start()
 
-    peers = [band_at(step) for step in range(1, bands)] + [dom_at(step) for step in range(1, domains)]
+    parity = lax.rem(band, 2)
+    chip = band - parity
+    across = {"band": band + 1 - 2 * parity}
+    onward = {"dom": lax.rem(dom + 2 * parity - 1 + domains, domains), "band": band + 1 - 2 * parity}
+    peers = [onward] + [band_at(step) for step in range(1, bands)] + [dom_at(step) for step in range(1, domains)]
     barrier = pltpu.get_barrier_semaphore()
     for peer in peers:
         pl.semaphore_signal(barrier, inc=1, device_id=peer, device_id_type=MESH)
@@ -114,24 +119,24 @@
             tv[o] = mm(small_eye, v[o].reshape(256, 128), NT).astype(BF16)
 
     for share in range(8):
-        span = slice(LANES * share, LANES * share + LANES)
-        tiles = mm(pm[...], tv[:, span, :].reshape(256, 256)).astype(BF16).reshape(LANES, 16, 256)
+        span = slice(HALF * share, HALF * share + HALF)
+        tiles = mm(pm[...], tv[:, span, :].reshape(256, 256)).astype(BF16).reshape(HALF, 16, 256)
         vt[0, span] = tiles[:, :, 0:128]
         vt[1, span] = tiles[:, :, 128:256]
     vt[:, 128 : 128 + REACH] = vt[:, 0:REACH]
 
     pl.semaphore_wait(barrier, len(peers))
 
-    parity = lax.rem(band, 2)
     a_copies, b_copies = [], []
     for step in range(1, bands):
         peer = band_at(step)
         other, side = peer["band"], lax.rem(peer["band"], 2)
+        start = HALF * (other - side)
         a_copies.append(send(
-            vt.at[side, pl.ds(LANES * other, LANES)], va.at[band, side, pl.ds(0, LANES)],
+            vt.at[side, pl.ds(start + HALF * side, HALF)], va.at[band, pl.ds(HALF * side, HALF)],
             a_send.at[step - 1], a_recv.at[step - 1], peer,
         ))
-    own = pltpu.make_async_copy(vt.at[:, pl.ds(LANES * band, LANES + REACH)], va.at[band], own_sem.at[0])
+    own = pltpu.make_async_copy(vt.at[parity, pl.ds(HALF * chip, LANES + REACH)], va.at[band], own_sem.at[0])
     own.start()
 
     def send_halos(k):
@@ -141,22 +146,12 @@
         )
 
     h_copies = [send_halos(1), send_halos(2)]
-    for step in range(1, bands):
-        peer = band_at(step)
-        other, side = peer["band"], lax.rem(peer["band"], 2)
-        b_copies.append(send(
-            vt.at[1 - side, pl.ds(LANES * other, LANES + REACH)], va.at[band, 1 - side],
-            b_send.at[0, step - 1], b_recv.at[0, step - 1], peer,
-        ))
-        b_copies.append(send(
-            vt.at[side, pl.ds(LANES * other + LANES, REACH)], va.at[band, side, pl.ds(LANES, REACH)],
-            b_send.at[1, step - 1], b_recv.at[1, step - 1], peer,
-        ))
-
-    onward = dom_at(2 * parity - 1)
-
     def forward(source, place):
-        return send(va.at[source, parity, pl.ds(0, LANES)], hb.at[source], f_send.at[place], f_recv.at[place], onward)
+        half = va.at[source, pl.ds(HALF * parity, HALF)]
+        return (
+            send(half, hb.at[source], f_send.at[0, place], f_recv.at[0, place], onward),
+            send(half, hc.at[source], f_send.at[1, place], f_recv.at[1, place], across),
+        )
 
     for load in loads:
         load.wait()
@@ -190,11 +185,24 @@
         send(q.at[0], rq.at[5], q_send.at[3], q_recv.at[3], dom_at(-2)),
     ]
 
+    for step in range(1, bands):
+        peer = band_at(step)
+        other, side = peer["band"], lax.rem(peer["band"], 2)
+        start = HALF * (other - side)
+        b_copies.append(send(
+            vt.at[side, pl.ds(start + HALF * (1 - side), HALF)], va.at[band, pl.ds(HALF * (1 - side), HALF)],
+            b_send.at[0, step - 1], b_recv.at[0, step - 1], peer,
+        ))
+        b_copies.append(send(
+            vt.at[side, pl.ds(start + LANES, REACH)], va.at[band, pl.ds(LANES, REACH)],
+            b_send.at[1, step - 1], b_recv.at[1, step - 1], peer,
+        ))
+
     own.wait()
-    f_copies = [forward(band, 0)]
+    f_copies = [*forward(band, 0)]
     for step, copy in enumerate(a_copies, 1):
         copy.wait_recv()
-        f_copies.append(forward(lax.rem(band - step + bands, bands), step))
+        f_copies += forward(lax.rem(band - step + bands, bands), step)
     lm[:, 0:256], lm[:, 256:512] = split(plane_matrix())
     zm[0:128], zm[128:256] = split(lane_matrix())
 
@@ -268,47 +276,49 @@
     finish(1)
     finish(2)
 
-    pott[...] = pot[...].reshape(256, 128).T
-    mb[0:128], mb[128:256] = split(boundary_matrix(parity))
-    gram[...] = jnp.zeros_like(gram)
-    for copy in b_copies:
-        copy.wait_recv()
-    h_copies += [send_halos(3), send_halos(4)]
-
-    @pl.loop(0, LANES, step=4)
-    def _(first):
-        lanes = [
-            jnp.concatenate([va[:, 0, first + i].reshape(128, 128), va[:, 1, first + i].reshape(128, 128)], axis=1)
-            for i in range(8)
-        ]
+    for group in range(2):
+        pott[group] = pot[4 * group : 4 * group + 4].reshape(128, 128).T
+    for place, side in ((0, 1 - parity), (256, parity)):
+        mb[place : place + 128], mb[place + 128 : place + 256] = split(boundary_matrix(side))
+    few_planes = jnp.concatenate([lm[0:128, 0:128], lm[0:128, 256:384]], axis=1)
+    for copy in n_copies:
+        copy.wait_recv()
+    gram[:, 0:128] = mm(ra[:, :, 0:128].reshape(128, 128), ra[:, :, 128:256].reshape(128, 128), NT)
+    gram[:, 128:768] = jnp.zeros((128, 640), F32)
+
+    def within(first):
+        lanes = [va[:, first + i].reshape(128, 128) for i in range(12)]
         images = []
-        for i in range(4):
-            weights = pott[pl.ds(LANES * band + first + i, 1), :]
-            image = mm(jnp.concatenate([lanes[i], lanes[i]], axis=1), lm[...], NT) + weights * lanes[i].astype(F32)
+        for i in range(8):
+            weights = pott[parity, pl.ds(HALF * chip + first + i, 1), :]
+            image = mm(jnp.concatenate([lanes[i], lanes[i]], axis=1), few_planes, NT) + weights * lanes[i].astype(F32)
             images.append(image.astype(BF16))
         rows = [jnp.concatenate(images, axis=1)]
-        rows += [jnp.concatenate(lanes[k : k + 4], axis=1) for k in range(1, 5)]
-        gram[:, 0:640] += mm(jnp.concatenate(lanes[0:4], axis=1), jnp.concatenate(rows, axis=0), NT)
-
+        rows += [jnp.concatenate(lanes[k : k + 8], axis=1) for k in range(1, 5)]
+        gram[:, 0:640] += mm(jnp.concatenate(lanes[0:8], axis=1), jnp.concatenate(rows, axis=0), NT)
+
+    within(HALF * parity)
+    for copy in b_copies:
+        copy.wait_recv()
+    h_copies += [send_halos(3), send_halos(4)]
+    for first in (HALF * parity + 8, HALF * (1 - parity), HALF * (1 - parity) + 8):
+        within(first)
     for copy in f_copies:
         copy.wait_recv()
 
-    @pl.loop(0, LANES, step=4)
+    @pl.loop(0, HALF, step=8)
     def _(first):
         near, far = [], []
-        for i in range(4):
-            near.append(va[:, 1 - parity, first + i].reshape(128, 128))
-            across = hb[:, first + i].reshape(128, 128)
-            far.append(mm(jnp.concatenate([across, across], axis=1), mb[...]).astype(BF16))
+        for i in range(8):
+            near.append(va[:, HALF * (1 - parity) + first + i].reshape(128, 128))
+            beyond, beside = hb[:, first + i].reshape(128, 128), hc[:, first + i].reshape(128, 128)
+            far.append(mm(jnp.concatenate([beyond, beyond, beside, beside], axis=1), mb[...]).astype(BF16))
         gram[:, 640:768] += mm(jnp.concatenate(near, axis=1), jnp.concatenate(far, axis=1), NT)
 
-    for copy in n_copies:
-        copy.wait_recv()
     once = gram[:, 640:768]
     for k in range(1, 5):
         once = once - 0.5 * STENCIL[k] * gram[:, 128 * k : 128 * k + 128]
-    nonlocal_part = mm(ra[:, :, 0:128].reshape(128, 128), ra[:, :, 128:256].reshape(128, 128), NT)
-    gram[:, 0:128] = gram[:, 0:128] + once + once.T + nonlocal_part
+    gram[:, 0:128] = gram[:, 0:128] + once + once.T
 
     s_copies = []
     for step in range(1, bands):
@@ -327,13 +337,10 @@
         for step in range(1, domains)
     ]
     finish(4)
-    leave = pltpu.make_async_copy(out, out_hbm, own_sem.at[1])
-    leave.start()
     for copy in d_copies:
         copy.wait_recv()
     gram_out[...] = jnp.sum(rd[...].astype(F32), axis=0) * (1.0 / (domains * 32768))
 
-    leave.wait()
     for copy in a_copies + b_copies + f_copies + q_copies + n_copies + s_copies + d_copies:
         copy.wait_send()
     for copies in h_copies:
@@ -341,40 +348,17 @@
             copy.wait_send()
 
 
-PARTS = 4
-
-
-def place(applied, gram, applied_out, gram_out, held, held_gram, come, go):
-    refs = [
-        (applied.at[pl.ds(16 // PARTS * part, 16 // PARTS)], held.at[pl.ds(16 // PARTS * part, 16 // PARTS)],
-         applied_out.at[pl.ds(16 // PARTS * part, 16 // PARTS)])
-        for part in range(PARTS)
-    ]
-    refs.append((gram, held_gram, gram_out))
-    arriving = [pltpu.make_async_copy(src, held_part, come.at[i]) for i, (src, held_part, _) in enumerate(refs)]
-    leaving = [pltpu.make_async_copy(held_part, dst, go.at[i]) for i, (_, held_part, dst) in enumerate(refs)]
-    for copy in arriving:
-        copy.start()
-    for first, second in zip(arriving, leaving):
-        first.wait()
-        second.start()
-    for copy in leaving:
-        copy.wait()
-
-
 def local(domains, bands, orbitals, potential, coupling, projectors, slot_atom, slot_domain_block, slot_count):
     vmem = pl.BlockSpec(memory_space=pltpu.VMEM)
     smem = pl.BlockSpec(memory_space=pltpu.SMEM)
     hbm = pl.BlockSpec(memory_space=pltpu.HBM)
     sums = bands + domains - 2
-    shapes = (jax.ShapeDtypeStruct((16, 8, 32, 128), BF16), jax.ShapeDtypeStruct((16, 128), F32))
-    results = pl.pallas_call(
+    return pl.pallas_call(
         functools.partial(kernel, domains, bands),
-        out_shape=shapes,
+        out_shape=(pltpu.VMEM((16, 8, 32, 128), BF16), pltpu.VMEM((16, 128), F32)),
         in_specs=[hbm, hbm, smem, hbm, hbm, hbm, smem],
-        out_specs=(hbm, vmem),
+        out_specs=(vmem, vmem),
         scratch_shapes=[
-            pltpu.VMEM((16, 8, 32, 128), BF16),
             pltpu.VMEM((16, 8, 32, 128), BF16),
             pltpu.VMEM((8, 32, 128), F32),
             pltpu.VMEM((256, 512), BF16),
@@ -382,8 +366,9 @@
             pltpu.VMEM((1, 256), jnp.int32),
             pltpu.VMEM((16, 128, 256), BF16),
             pltpu.VMEM((2, 128 + REACH, 16, 128), BF16),
-            pltpu.VMEM((8, 2, LANES + REACH, 16, 128), BF16),
-            pltpu.VMEM((8, LANES, 16, 128), BF16),
+            pltpu.VMEM((8, LANES + REACH, 16, 128), BF16),
+            pltpu.VMEM((8, HALF, 16, 128), BF16),
+            pltpu.VMEM((8, HALF, 16, 128), BF16),
             pltpu.VMEM((4, 16, 32, 128), BF16),
             pltpu.VMEM((4, 16, 32, 128), BF16),
             pltpu.VMEM((16, 8, 32, 128), F32),
@@ -397,8 +382,8 @@
             pltpu.VMEM((256, 256), BF16),
             pltpu.VMEM((256, 512), BF16),
             pltpu.VMEM((256, 128), BF16),
-            pltpu.VMEM((256, 128), BF16),
-            pltpu.VMEM((128, 256), F32),
+            pltpu.VMEM((512, 128), BF16),
+            pltpu.VMEM((2, 128, 128), F32),
             pltpu.VMEM((128, 256), BF16),
             pltpu.VMEM((8, 16, 256), BF16),
             pltpu.VMEM((128, 768), F32),
@@ -409,8 +394,8 @@
             pltpu.SemaphoreType.DMA((7,)),
             pltpu.SemaphoreType.DMA((2, 7)),
             pltpu.SemaphoreType.DMA((2, 7)),
-            pltpu.SemaphoreType.DMA((8,)),
-            pltpu.SemaphoreType.DMA((8,)),
+            pltpu.SemaphoreType.DMA((2, 8)),
+            pltpu.SemaphoreType.DMA((2, 8)),
             pltpu.SemaphoreType.DMA((2, 4)),
             pltpu.SemaphoreType.DMA((2, 4)),
             pltpu.SemaphoreType.DMA((4,)),
@@ -428,19 +413,6 @@
         orbitals, potential, coupling, projectors,
         slot_atom.reshape(1, -1), slot_domain_block.reshape(1, -1), slot_count,
     )
-    return pl.pallas_call(
-        place,
-        out_shape=shapes,
-        in_specs=[hbm, hbm],
-        out_specs=(hbm, hbm),
-        scratch_shapes=[
-            pltpu.VMEM((16, 8, 32, 128), BF16),
-            pltpu.VMEM((16, 128), F32),
-            pltpu.SemaphoreType.DMA((PARTS + 1,)),
-            pltpu.SemaphoreType.DMA((PARTS + 1,)),
-        ],
-        compiler_params=pltpu.CompilerParams(vmem_limit_bytes=62 * 1024 * 1024),
-    )(*results)
 
 
 def solution(mesh):

time: 48.6 us -> 47 us (0.967)
  Pallas kernels: 47.1 us -> 44 us
  local copies, waits for them, and re-layouts: 0 us -> 1.57 us
    pallas_call x2 -> x1, Pallas kernels: 47.1 us -> 44 us  [local(): pl.pallas_call(functools.partial(kernel, domains, bands), out_shape=(pltp...]
    unnamed x0 -> x2, local copies, waits for them, and re-layouts: none -> 1.57 us
where the time goes in v4:
time: 47 us; the launch traced here: 46.8 us
  Pallas kernels  44 us (94%)
  local copies, waits for them, and re-layouts  1.57 us (3%)
  between operations  1.29 us (3%)
    pallas_call x1, Pallas kernels, local(): pl.pallas_call(functools.partial(kernel, domains, bands), out_shape=(pltp...  44 us
    unnamed x2, local copies, waits for them, and re-layouts  1.57 us

profile of v4, /device:TPU:6, one launch (start us, length us, event | category | flops | bytes accessed | tf_op | source)
XLA Modules:
  0.0 46.8 jit_solution(2952478384787087901)
XLA Ops:
  1.3 44.0 %shard_map.86 = (bf16[16,8,32,128]{3,2,1,0:T(8,128)(2,1)S(1)}, f32[16,128]{1,0:T(8,128)S(1)}) custom-call(bf16[16,8,32,128]{3,2,1,0:T(8,128)(2,1)} %v_in.1, f32[8,32,128]{2,1,0:T(8,128)} %pot_in.1, f32[8,8]{1,0:T(8,128)} %coupling.1, bf16[256,512]{1,0:T(8,128)(2,1)} %proj_in.1, s32[1,256]{1,0:T(1,128)} %bitcast.2, s32[1,256]{1,0:T(1,128)} %bitcast.3, ...), custom_call_target="tpu_custom_call" | custom-call | tf_op jit(solution)/shard_map/pallas_call | solution.py:356
  45.3 1.0 %copy.11 = bf16[16,8,32,128]{3,2,1,0:T(8,128)(2,1)} copy(bf16[16,8,32,128]{3,2,1,0:T(8,128)(2,1)S(1)} %get-tuple-element.2) | data formatting | bytes 2097152
  46.2 0.6 %copy.12 = f32[16,128]{1,0:T(8,128)} copy(f32[16,128]{1,0:T(8,128)S(1)} %get-tuple-element.3) | data formatting | bytes 16384

commit v5 on v4

--- a/solution.py
+++ b/solution.py
@@ -328,31 +328,34 @@
             s_send.at[step - 1], s_recv.at[step - 1], peer,
         ))
     rb[band] = gram[pl.ds(pl.multiple_of(band * 16, 16), 16), 0:128]
+    for copy in s_copies:
+        copy.wait_recv()
+    rd[dom] = jnp.sum(rb[...], axis=0).astype(BF16)
+    for step in range(1, domains):
+        send(rd.at[dom], rd.at[dom], s_send.at[bands - 1], s_recv.at[bands - 1], dom_at(step))
     finish(3)
-    for copy in s_copies:
-        copy.wait_recv()
-    rd[dom] = jnp.sum(rb[...], axis=0).astype(BF16)
-    d_copies = [
-        send(rd.at[dom], rd.at[dom], s_send.at[bands - 2 + step], s_recv.at[bands - 2 + step], dom_at(step))
-        for step in range(1, domains)
-    ]
     finish(4)
-    for copy in d_copies:
-        copy.wait_recv()
-    gram_out[...] = jnp.sum(rd[...].astype(F32), axis=0) * (1.0 / (domains * 32768))
-
-    for copy in a_copies + b_copies + f_copies + q_copies + n_copies + s_copies + d_copies:
+    for copy in a_copies + b_copies + f_copies + q_copies + n_copies + s_copies:
         copy.wait_send()
     for copies in h_copies:
         for copy in copies:
             copy.wait_send()
+    others = rd.at[pl.ds(0, domains - 1)]
+    every = pltpu.make_async_remote_copy(
+        src_ref=others, dst_ref=others, send_sem=s_send.at[bands - 1], recv_sem=s_recv.at[bands - 1],
+        device_id=dom_at(1), device_id_type=MESH,
+    )
+    every.wait_recv()
+    gram_out[...] = jnp.sum(rd[...].astype(F32), axis=0) * (1.0 / (domains * 32768))
+
+    every.wait_send()
 
 
 def local(domains, bands, orbitals, potential, coupling, projectors, slot_atom, slot_domain_block, slot_count):
     vmem = pl.BlockSpec(memory_space=pltpu.VMEM)
     smem = pl.BlockSpec(memory_space=pltpu.SMEM)
     hbm = pl.BlockSpec(memory_space=pltpu.HBM)
-    sums = bands + domains - 2
+    sums = bands
     return pl.pallas_call(
         functools.partial(kernel, domains, bands),
         out_shape=(pltpu.VMEM((16, 8, 32, 128), BF16), pltpu.VMEM((16, 128), F32)),

time: 47 us -> 46.2 us (0.983)
  Pallas kernels: 44 us -> 43.2 us
    pallas_call x1, Pallas kernels: 44 us -> 43.2 us  [local(): pl.pallas_call(functools.partial(kernel, domains, bands), out_shape=(pltp...]
where the time goes in v5:
time: 46.2 us; the launch traced here: 46.1 us
  Pallas kernels  43.2 us (94%)
  local copies, waits for them, and re-layouts  1.57 us (3%)
  between operations  1.29 us (3%)
    pallas_call x1, Pallas kernels, local(): pl.pallas_call(functools.partial(kernel, domains, bands), out_shape=(pltp...  43.2 us
    unnamed x2, local copies, waits for them, and re-layouts  1.57 us

profile of v5, /device:TPU:6, one launch (start us, length us, event | category | flops | bytes accessed | tf_op | source)
XLA Modules:
  0.0 46.1 jit_solution(4980079062466963723)
XLA Ops:
  1.3 43.2 %shard_map.86 = (bf16[16,8,32,128]{3,2,1,0:T(8,128)(2,1)S(1)}, f32[16,128]{1,0:T(8,128)S(1)}) custom-call(bf16[16,8,32,128]{3,2,1,0:T(8,128)(2,1)} %v_in.1, f32[8,32,128]{2,1,0:T(8,128)} %pot_in.1, f32[8,8]{1,0:T(8,128)} %coupling.1, bf16[256,512]{1,0:T(8,128)(2,1)} %proj_in.1, s32[1,256]{1,0:T(1,128)} %bitcast.2, s32[1,256]{1,0:T(1,128)} %bitcast.3, ...), custom_call_target="tpu_custom_call" | custom-call | tf_op jit(solution)/shard_map/pallas_call | solution.py:359
  44.5 1.0 %copy.11 = bf16[16,8,32,128]{3,2,1,0:T(8,128)(2,1)} copy(bf16[16,8,32,128]{3,2,1,0:T(8,128)(2,1)S(1)} %get-tuple-element.2) | data formatting | bytes 2097152
  45.5 0.6 %copy.12 = f32[16,128]{1,0:T(8,128)} copy(f32[16,128]{1,0:T(8,128)S(1)} %get-tuple-element.3) | data formatting | bytes 16384

commit v6 on v5

--- a/solution.py
+++ b/solution.py
@@ -138,6 +138,11 @@
         ))
     own = pltpu.make_async_copy(vt.at[parity, pl.ds(HALF * chip, LANES + REACH)], va.at[band], own_sem.at[0])
     own.start()
+
+    def together(refs, send_sem, recv_sem):
+        return pltpu.make_async_remote_copy(
+            src_ref=refs, dst_ref=refs, send_sem=send_sem, recv_sem=recv_sem, device_id=dom_at(1), device_id_type=MESH
+        )
 
     def send_halos(k):
         return (
@@ -191,11 +196,11 @@
         start = HALF * (other - side)
         b_copies.append(send(
             vt.at[side, pl.ds(start + HALF * (1 - side), HALF)], va.at[band, pl.ds(HALF * (1 - side), HALF)],
-            b_send.at[0, step - 1], b_recv.at[0, step - 1], peer,
+            b_send.at[0], b_recv.at[0], peer,
         ))
         b_copies.append(send(
             vt.at[side, pl.ds(start + LANES, REACH)], va.at[band, pl.ds(LANES, REACH)],
-            b_send.at[1, step - 1], b_recv.at[1, step - 1], peer,
+            b_send.at[1], b_recv.at[1], peer,
         ))
 
     own.wait()
@@ -298,6 +303,10 @@
         gram[:, 0:640] += mm(jnp.concatenate(lanes[0:8], axis=1), jnp.concatenate(rows, axis=0), NT)
 
     within(HALF * parity)
+    b_copies = [
+        together(va.at[pl.ds(0, bands - 1), pl.ds(0, HALF)], b_send.at[0], b_recv.at[0]),
+        together(va.at[pl.ds(0, bands - 1), pl.ds(LANES, REACH)], b_send.at[1], b_recv.at[1]),
+    ]
     for copy in b_copies:
         copy.wait_recv()
     h_copies += [send_halos(3), send_halos(4)]
@@ -325,14 +334,14 @@
         peer = band_at(step)
         s_copies.append(send(
             gram.at[pl.ds(pl.multiple_of(peer["band"] * 16, 16), 16), pl.ds(0, 128)], rb.at[band],
-            s_send.at[step - 1], s_recv.at[step - 1], peer,
+            s_send.at[0], s_recv.at[0], peer,
         ))
     rb[band] = gram[pl.ds(pl.multiple_of(band * 16, 16), 16), 0:128]
-    for copy in s_copies:
-        copy.wait_recv()
+    s_copies = [together(rb.at[pl.ds(0, bands - 1)], s_send.at[0], s_recv.at[0])]
+    s_copies[0].wait_recv()
     rd[dom] = jnp.sum(rb[...], axis=0).astype(BF16)
     for step in range(1, domains):
-        send(rd.at[dom], rd.at[dom], s_send.at[bands - 1], s_recv.at[bands - 1], dom_at(step))
+        send(rd.at[dom], rd.at[dom], s_send.at[1], s_recv.at[1], dom_at(step))
     finish(3)
     finish(4)
     for copy in a_copies + b_copies + f_copies + q_copies + n_copies + s_copies:
@@ -342,7 +351,7 @@
             copy.wait_send()
     others = rd.at[pl.ds(0, domains - 1)]
     every = pltpu.make_async_remote_copy(
-        src_ref=others, dst_ref=others, send_sem=s_send.at[bands - 1], recv_sem=s_recv.at[bands - 1],
+        src_ref=others, dst_ref=others, send_sem=s_send.at[1], recv_sem=s_recv.at[1],
         device_id=dom_at(1), device_id_type=MESH,
     )
     every.wait_recv()
@@ -355,7 +364,7 @@
     vmem = pl.BlockSpec(memory_space=pltpu.VMEM)
     smem = pl.BlockSpec(memory_space=pltpu.SMEM)
     hbm = pl.BlockSpec(memory_space=pltpu.HBM)
-    sums = bands
+    sums = 2
     return pl.pallas_call(
         functools.partial(kernel, domains, bands),
         out_shape=(pltpu.VMEM((16, 8, 32, 128), BF16), pltpu.VMEM((16, 128), F32)),
@@ -395,8 +404,8 @@
             pltpu.SemaphoreType.DMA((8,)),
             pltpu.SemaphoreType.DMA((7,)),
             pltpu.SemaphoreType.DMA((7,)),
-            pltpu.SemaphoreType.DMA((2, 7)),
-            pltpu.SemaphoreType.DMA((2, 7)),
+            pltpu.SemaphoreType.DMA((2,)),
+            pltpu.SemaphoreType.DMA((2,)),
             pltpu.SemaphoreType.DMA((2, 8)),
             pltpu.SemaphoreType.DMA((2, 8)),
             pltpu.SemaphoreType.DMA((2, 4)),

time: 46.2 us -> 45.9 us (level)
  no operation moved by 1% of the time
where the time goes in v6:
time: 45.9 us; the launch traced here: 45.7 us
  Pallas kernels  42.9 us (93%)
  local copies, waits for them, and re-layouts  1.57 us (3%)
  between operations  1.29 us (3%)
    pallas_call x1, Pallas kernels, local(): pl.pallas_call(functools.partial(kernel, domains, bands), out_shape=(pltp...  42.9 us
    unnamed x2, local copies, waits for them, and re-layouts  1.57 us

profile of v6, /device:TPU:6, one launch (start us, length us, event | category | flops | bytes accessed | tf_op | source)
XLA Modules:
  0.0 45.7 jit_solution(17203329688898279203)
XLA Ops:
  1.3 42.9 %shard_map.86 = (bf16[16,8,32,128]{3,2,1,0:T(8,128)(2,1)S(1)}, f32[16,128]{1,0:T(8,128)S(1)}) custom-call(bf16[16,8,32,128]{3,2,1,0:T(8,128)(2,1)} %v_in.1, f32[8,32,128]{2,1,0:T(8,128)} %pot_in.1, f32[8,8]{1,0:T(8,128)} %coupling.1, bf16[256,512]{1,0:T(8,128)(2,1)} %proj_in.1, s32[1,256]{1,0:T(1,128)} %bitcast.2, s32[1,256]{1,0:T(1,128)} %bitcast.3, ...), custom_call_target="tpu_custom_call" | custom-call | tf_op jit(solution)/shard_map/pallas_call | solution.py:368
  44.2 1.0 %copy.11 = bf16[16,8,32,128]{3,2,1,0:T(8,128)(2,1)} copy(bf16[16,8,32,128]{3,2,1,0:T(8,128)(2,1)S(1)} %get-tuple-element.2) | data formatting | bytes 2097152
  45.1 0.6 %copy.12 = f32[16,128]{1,0:T(8,128)} copy(f32[16,128]{1,0:T(8,128)S(1)} %get-tuple-element.3) | data formatting | bytes 16384
